TPU v7x, 32 devices: a whole 2x2x4 slice. The times are simulated.
32 devices in a mesh: seq: 8 (over y, x, core), tp: 4 (over z).
Axes of the slice: x: 2, y: 2, z: 4, core: 2. Of those that a mesh axis runs over, the one named last changes fastest.
Arguments:
- head_inputs: bfloat16 [8192, 6144], P('seq', 'tp'), may hold values from -2 to 2
- write_keys: bfloat16 [8192, 128], P(('seq', 'tp')), may hold values from -1.796875 to 1.796875
- read_queries: bfloat16 [8192, 128], P(('seq', 'tp')), may hold values from -1.796875 to 1.796875
- log_decay: float32 [96, 8192], P('tp', 'seq'), may hold values from -0.7 to 0
- skip_gain: float32 [96], P('tp'), may hold values from 0.5 to 1.5
- out_grad: bfloat16 [8192, 6144], P('seq', 'tp'), may hold values from -2 to 2
Outputs:
- mixed_out: bfloat16 [8192, 6144], P('seq', 'tp')
- input_grad: bfloat16 [8192, 6144], P('seq', 'tp')
- write_grad: bfloat16 [8192, 128], P(('seq', 'tp'))
- read_grad: bfloat16 [8192, 128], P(('seq', 'tp'))
All inputs are finite; a program needn't handle non-finite values.
Results may differ from a plain program's by a relative error of at most 0.015.
Values may be sent and summed in bfloat16 or wider, within the bound.
A program may use at most 128 MiB of HBM per device.

v0:
```python
import jax
import jax.numpy as jnp
from jax import lax
from jax.sharding import PartitionSpec as P

HEADDIM = 64
STATE = 128
BLK = 512


def entering(x, axis, combine, identity, reverse):
    count, position = (lax.axis_size(axis), lax.axis_index(axis))
    everything = jax.tree.map(
        lambda part, kind: lax.all_gather(part.astype(kind), axis), x, (jnp.bfloat16, jnp.bfloat16)
    )
    start = jax.tree.map(
        lambda part, zero: jnp.broadcast_to(jnp.asarray(zero, part.dtype), part.shape), x, identity
    )

    def step(k, before):
        at = count - 1 - k if reverse else k
        reached = at > position if reverse else at < position
        new = combine(
            before, jax.tree.map(lambda part, own: part[at].astype(own.dtype), everything, x)
        )
        return jax.tree.map(lambda a, b: jnp.where(reached, a, b), new, before)

    return lax.fori_loop(0, count, step, start)


def repeat_heads(values):
    return jnp.repeat(values, HEADDIM, axis=-1)


def chain_join(earlier, later):
    early_log, early_state = earlier
    late_log, late_state = later
    return (
        early_log + late_log,
        jnp.exp(repeat_heads(late_log))[None, :] * early_state + late_state,
    )


def carry_step(state, inputs):
    summary, factor = inputs
    return (factor[None, :] * state + summary, state)


def local(head_inputs, write_keys, read_queries, log_decay, skip_gain, out_grad):
    tok_count = head_inputs.shape[0]
    width = head_inputs.shape[1]
    heads = width // HEADDIM
    blocks = tok_count // BLK
    key_full, query_full = (
        lax.all_gather(write_keys, "tp", axis=0, tiled=True),
        lax.all_gather(read_queries, "tp", axis=0, tiled=True),
    )
    input_blocks = head_inputs.reshape(blocks, BLK, width)
    grad_blocks = out_grad.reshape(blocks, BLK, width)
    key_blocks = key_full.reshape(blocks, BLK, STATE)
    query_blocks = query_full.reshape(blocks, BLK, STATE)
    running = jnp.cumsum(log_decay.reshape(heads, blocks, BLK), axis=2).transpose(1, 0, 2)
    block_logs = running[:, :, -1]
    to_end = repeat_heads(jnp.exp(block_logs[:, :, None] - running).transpose(0, 2, 1))
    from_start = repeat_heads(jnp.exp(running).transpose(0, 2, 1))
    scaled_inputs = (input_blocks * to_end).astype(jnp.bfloat16)
    scaled_grads = (grad_blocks * from_start).astype(jnp.bfloat16)
    state_sums = jnp.einsum(
        "bln,blc->bnc", key_blocks, scaled_inputs, preferred_element_type=jnp.float32
    )
    cotangent_sums = jnp.einsum(
        "bln,blc->bnc", query_blocks, scaled_grads, preferred_element_type=jnp.float32
    )
    block_factor = jnp.exp(repeat_heads(block_logs))
    empty = jnp.zeros((STATE, width), jnp.float32)
    local_end, prefix = lax.scan(carry_step, empty, (state_sums, block_factor))
    local_start, suffix = lax.scan(carry_step, empty, (cotangent_sums, block_factor), reverse=True)
    total_log = jnp.sum(block_logs, axis=0)
    through = jnp.cumsum(block_logs, axis=0)
    into_block = jnp.exp(repeat_heads(through - block_logs))
    after_block = jnp.exp(repeat_heads(total_log[None, :] - through))
    state_enter = entering(
        (total_log, local_end), "seq", chain_join, (jnp.zeros_like(total_log), empty), False
    )[1]
    cot_enter = entering(
        (total_log, local_start), "seq", chain_join, (jnp.zeros_like(total_log), empty), True
    )[1]
    state_blocks = (prefix + into_block[:, None, :] * state_enter[None]).astype(jnp.bfloat16)
    cot_blocks = (suffix + after_block[:, None, :] * cot_enter[None]).astype(jnp.bfloat16)
    skip_cols = repeat_heads(skip_gain)
    order = jnp.arange(BLK)
    lower = order[:, None] >= order[None, :]

    def one_block(pack):
        (
            running_b,
            input_b,
            grad_b,
            key_b,
            query_b,
            state_b,
            cot_b,
            scaled_in_b,
            scaled_grad_b,
            to_end_b,
            from_start_b,
        ) = pack
        gram = jnp.dot(query_b, key_b.T, preferred_element_type=jnp.float32)
        spread = running_b[:, :, None] - running_b[:, None, :]
        decay = jnp.exp(jnp.where(lower[None], spread, -jnp.inf))
        weights = (decay * gram[None]).astype(jnp.bfloat16)
        input_heads = input_b.reshape(BLK, heads, HEADDIM)
        grad_heads = grad_b.reshape(BLK, heads, HEADDIM)
        forward_part = jnp.einsum(
            "hts,shp->thp", weights, input_heads, preferred_element_type=jnp.float32
        ).reshape(BLK, width)
        mixed = (
            forward_part
            + jnp.dot(query_b, state_b, preferred_element_type=jnp.float32) * from_start_b
            + skip_cols[None, :] * input_b
        )
        backward_part = jnp.einsum(
            "hts,thp->shp", weights, grad_heads, preferred_element_type=jnp.float32
        ).reshape(BLK, width)
        grad_in = (
            backward_part
            + jnp.dot(key_b, cot_b, preferred_element_type=jnp.float32) * to_end_b
            + skip_cols[None, :] * grad_b
        )
        pairs = jnp.einsum(
            "thp,shp->hts", grad_heads, input_heads, preferred_element_type=jnp.float32
        )
        mixer = jnp.sum(decay * pairs, axis=0)
        key_grad = jnp.dot(mixer.T, query_b.astype(jnp.float32), precision=lax.Precision.HIGHEST)
        key_grad = key_grad + jnp.einsum(
            "lc,nc->ln", scaled_in_b, cot_b, preferred_element_type=jnp.float32
        )
        query_grad = jnp.dot(mixer, key_b.astype(jnp.float32), precision=lax.Precision.HIGHEST)
        query_grad = query_grad + jnp.einsum(
            "lc,nc->ln", scaled_grad_b, state_b, preferred_element_type=jnp.float32
        )
        return (mixed.astype(jnp.bfloat16), grad_in.astype(jnp.bfloat16), key_grad, query_grad)

    mixed_blocks, grad_blocks_out, key_grads, query_grads = lax.map(
        one_block,
        (
            running,
            input_blocks,
            grad_blocks,
            key_blocks,
            query_blocks,
            state_blocks,
            cot_blocks,
            scaled_inputs,
            scaled_grads,
            to_end,
            from_start,
        ),
    )
    mixed_out = mixed_blocks.reshape(tok_count, width)
    input_grad = grad_blocks_out.reshape(tok_count, width)
    summed = (
        lax.psum_scatter(
            key_grads.reshape(tok_count, STATE).astype(jnp.bfloat16),
            "tp",
            scatter_dimension=0,
            tiled=True,
        ).astype(jnp.float32),
        lax.psum_scatter(
            query_grads.reshape(tok_count, STATE).astype(jnp.bfloat16),
            "tp",
            scatter_dimension=0,
            tiled=True,
        ).astype(jnp.float32),
    )
    return (mixed_out, input_grad, summed[0].astype(jnp.bfloat16), summed[1].astype(jnp.bfloat16))


def solution(mesh):
    in_specs = (
        P("seq", "tp"),
        P(("seq", "tp"), None),
        P(("seq", "tp"), None),
        P("tp", "seq"),
        P("tp"),
        P("seq", "tp"),
    )
    out_specs = (P("seq", "tp"), P("seq", "tp"), P(("seq", "tp"), None), P(("seq", "tp"), None))
    return jax.shard_map(local, mesh=mesh, in_specs=in_specs, out_specs=out_specs, check_vma=False)
```

profile of v0, /device:TPU:0, one launch (start us, length us, event | category | flops | bytes accessed | tf_op | source)
XLA Modules:
  0.0 304.2 jit_solution(1887035909628612947)
XLA Ops:
  8.2 2.3 reduce-window.6
  11.4 15.8 %all_gather.24 = bf16[1024,128]{1,0:T(8,128)(2,1)S(1)} all-gather(bf16[256,128]{1,0:T(8,128)(2,1)} %param.18), channel_id=1, replica_groups=mesh['seq'=8,'tp'=4] {'tp'}, dimensions={0}, use_global_device_ids=true | all-gather | bytes 327680 | tf_op jit(solution)/shard_map/all_gather | solution.py:56
  27.3 4.6 %copy.47 = bf16[2,512,1536]{1,2,0:T(8,128)(2,1)} copy(bf16[2,512,1536]{2,1,0:T(8,128)(2,1)} %bitcast.239) | data formatting | bytes 6291456 | tf_op jit(solution)/shard_map/reshape | solution.py:59
  31.9 2.5 multiply_convert_fusion.3
  34.4 2.2 convolution_bitcast_fusion
  38.0 5.5 %while.80 = (s32[]{:T(128)}, f32[128,1536]{1,0:T(8,128)S(1)}, f32[2,128,1536]{2,1,0:T(8,128)}, f32[2,1536]{1,0:T(2,128)S(1)}, f32[2,128,1536]{1,2,0:T(8,128)}, /*index=5*/s32[]{:T(128)}, s32[]{:T(128)}) while((s32[]{:T(128)}, f32[128,1536]{1,0:T(8,128)S(1)}, f32[2,128,1536]{2,1,0:T(8,128)}, f32[2,1536]{1,0:T(2,128)S(1)}, ...), condition=%wide.region_9.10_spmd.clone, body=%wide.region_8.9_spmd.clone.sunk | while | flops 786436 | bytes 7096440 | solution.py:77
  44.4 3.4 %broadcast_in_dim.98 = f32[2,512,24,64]{1,3,2,0:T(8,128)} broadcast(f32[2,512,24]{1,2,0:T(8,128)S(1)} %get-tuple-element.720), dimensions={0,1,2} | broadcast | bytes 6389760 | tf_op jit(solution)/shard_map/broadcast_in_dim | solution.py:32
  47.8 6.6 %copy.44 = f32[2,512,1536]{2,1,0:T(8,128)} copy(f32[2,512,1536]{1,2,0:T(8,128)} %bitcast.248) | data formatting | bytes 12582912 | tf_op jit(solution)/shard_map/reshape | solution.py:32
  54.5 15.1 %all_gather.25 = bf16[1024,128]{1,0:T(8,128)(2,1)} all-gather(bf16[256,128]{1,0:T(8,128)(2,1)S(1)} %copy-done.21), channel_id=1, replica_groups=mesh['seq'=8,'tp'=4] {'tp'}, dimensions={0}, use_global_device_ids=true | all-gather | bytes 327680 | tf_op jit(solution)/shard_map/all_gather | solution.py:55
  69.6 4.8 %multiply_convert_fusion.4 = bf16[2,512,1536]{2,1,0:T(8,128)(2,1)S(1)} fusion(f32[2,512,1536]{2,1,0:T(8,128)} %copy.44, bf16[2,512,1536]{2,1,0:T(8,128)(2,1)} %bitcast), kind=kLoop, calls=%fused_computation.95 | loop fusion | flops 4718592 | bytes 12582912 | tf_op jit(solution)/shard_map/convert_element_type | solution.py:66
  74.4 3.6 %convolution_bitcast_fusion.1 = f32[2,128,1536]{1,2,0:T(8,128)} fusion(bf16[2,512,1536]{2,1,0:T(8,128)(2,1)S(1)} %multiply_convert_fusion.4, bf16[2,512,128]{2,1,0:T(8,128)(2,1)} %bitcast.4), kind=kOutput, calls=%fused_computation.97 | convolution fusion | flops 402653184 | bytes 4980736 | tf_op jit(solution)/shard_map/bln,blc->bnc/dot_general | solution.py:68
  79.3 5.4 %while.78 = (s32[]{:T(128)}, f32[128,1536]{1,0:T(8,128)S(1)}, f32[2,128,1536]{2,1,0:T(8,128)}, f32[2,1536]{1,0:T(2,128)S(1)}, f32[2,128,1536]{1,2,0:T(8,128)}, /*index=5*/s32[]{:T(128)}, s32[]{:T(128)}) while((s32[]{:T(128)}, f32[128,1536]{1,0:T(8,128)S(1)}, f32[2,128,1536]{2,1,0:T(8,128)}, f32[2,1536]{1,0:T(2,128)S(1)}, ...), condition=%wide.region_3.4_spmd.clone, body=%wide.region_2.3_spmd.clone.sunk | while | flops 786435 | bytes 7096428 | solution.py:76
  87.3 11.9 %all-reduce = bf16[192]{0:T(256)(128)(2,1)S(1)} all-reduce(bf16[192]{0:T(256)(128)(2,1)S(1)} %dynamic-update-slice), channel_id=2, replica_groups=mesh['seq'=8,'tp'=4] {'seq'}, use_global_device_ids=true, to_apply=%add | all-reduce | flops 192 | bytes 768
  99.6 13.5 %while.81 = (s32[]{:T(128)}, f32[128,1536]{1,0:T(8,128)S(1)}, s32[]{:T(128)}, bf16[8,24]{1,0:T(8,128)(2,1)S(1)}, bf16[8,128,1536]{2,1,0:T(8,128)(2,1)}, /*index=5*/s32[]{:T(128)}, s32[]{:T(128)}, s32[]{:T(128)}, s32[]{:T(128)}) while((s32[]{:T(128)}, f32[128,1536]{1,0:T(8,128)S(1)}, s32[]{:T(128)}, ...), condition=%wide.region_11.12_spmd.clone, body=%wide.region_10.11_spmd.clone.sunk | while | flops 983072 | bytes 1991071 | solution.py:28
  106.5 1.6 fusion.154
  113.2 6.0 %all-gather.6.cloned.1.call-done = bf16[1024,1536]{1,0:T(8,128)(2,1)} async-done(((bf16[128,1536]{1,0:T(8,128)(2,1)}), bf16[1024,1536]{1,0:T(8,128)(2,1)}) %all-gather.6.cloned.1.call-update) | async-done | bytes 3145744 | tf_op jit(solution)/shard_map/all_gather | solution.py:14
  119.2 13.3 %while.79 = (s32[]{:T(128)}, f32[128,1536]{1,0:T(8,128)S(1)}, s32[]{:T(128)}, bf16[8,24]{1,0:T(8,128)(2,1)S(1)}, bf16[8,128,1536]{2,1,0:T(8,128)(2,1)}, /*index=5*/s32[]{:T(128)}, s32[]{:T(128)}) while((s32[]{:T(128)}, f32[128,1536]{1,0:T(8,128)S(1)}, s32[]{:T(128)}, bf16[8,24]{1,0:T(8,128)(2,1)S(1)}, ...), condition=%wide.region_7.8_spmd.clone, body=%wide.region_6.7_spmd.clone.sunk | while | flops 983068 | bytes 1991009 | solution.py:28
  132.6 2.6 add_convert_fusion
  136.4 3.4 %broadcast_in_dim.100 = f32[2,512,24,64]{1,3,2,0:T(8,128)} broadcast(f32[2,512,24]{1,2,0:T(8,128)S(1)} %copy-done.18), dimensions={0,1,2} | broadcast | bytes 6389760 | tf_op jit(solution)/shard_map/broadcast_in_dim | solution.py:32
  139.8 117.3 %while.77 = (s32[]{:T(128)}, bf16[2,512,1536]{2,1,0:T(8,128)(2,1)}, bf16[2,512,1536]{2,1,0:T(8,128)(2,1)}, bf16[2,512,128]{2,1,0:T(8,128)(2,1)}, bf16[2,512,128]...) while((s32[]{:T(128)}, bf16[2,512,1536]{2,1,0:T(8,128)(2,1)}, ...), condition=%wide.region_14.15_spmd.clone, body=%wide.region_12.14_spmd.clone.sunk | while | flops 4178706432 | bytes 159801088 | solution.py:144
  141.4 2.2 fusion.144
  143.5 2.2 constant_dynamic-slice_fusion.10
  145.7 2.4 copy.70
  148.1 2.1 constant_dynamic-slice_fusion.9
  151.8 1.6 copy.71
  153.4 9.2 %multiply_reduce_fusion.2 = f32[512,512]{1,0:T(8,128)S(1)} fusion(f32[24,512]{1,0:T(8,128)} %dynamic-slice_bitcast_fusion.2, pred[512,512]{1,0:T(8,128)(4,1)} %iota_compare_fusion.2, bf16[512,24,64]{0,2,1:T(8,128)(2,1)} %bitcast.246, bf16[512,24,64]{0,2,1:T(8,128)(2,1)S(1)} %bitcast.244), kind=kOutput, calls=%fused_computation.2.clone.1 | convolution fusion | flops 830210048 | bytes 4505600 | tf_op jit(solution)/shard_map/while/body/eval_jaxpr/thp,shp->hts/dot_general | solution.py:130
  162.6 1.7 fusion.151
  167.3 7.8 %fusion.147 = f32[24,64,512]{2,1,0:T(8,128)} fusion(bf16[512,24,64]{0,2,1:T(8,128)(2,1)S(1)} %bitcast.247, f32[512,512]{1,0:T(8,128)S(1)} %copy-done.7, f32[24,512]{1,0:T(8,128)S(1)} %copy-done.15, pred[512,512]{1,0:T(8,128)(4,1)S(1)} %copy-done.12), kind=kOutput, calls=%fused_computation.5.clone.1 | convolution fusion | flops 830472192 | bytes 6078464 | tf_op jit(solution)/shard_map/while/body/eval_jaxpr/hts,thp->shp/dot_general | solution.py:122
  175.2 2.4 copy.72
  177.6 4.5 %fusion.148 = bf16[2,512,1536]{2,1,0:T(8,128)(2,1)} fusion(bf16[2,512,1536]{2,1,0:T(8,128)(2,1)} %get-tuple-element.1065, s32[]{:T(128)S(6)} %copy.117, f32[512,1536]{1,0:T(8,128)S(1)} %copy.72, f32[2,512,1536]{2,1,0:T(8,128)} %get-tuple-element.1094, f32[1536]{0:T(1024)S(1)} %mul.282, bf16[2,128,1536]{2,1,0:T(8,128)(2,1)} %get-tuple-element.1093, ...), kind=kOutput, calls=%fused_computation.30.clone.1 | convolution fusion | flops 206045184 | bytes 9969152 | tf_op jit(solution)/shard_map/while/body/eval_jaxpr/dot_general | solution.py:127
  182.1 8.3 %fusion.145 = f32[24,64,512]{2,1,0:T(8,128)} fusion(bf16[512,24,64]{0,2,1:T(8,128)(2,1)S(1)} %bitcast.245, f32[512,512]{1,0:T(8,128)S(1)} %copy-done.8, f32[24,512]{1,0:T(8,128)S(1)} %copy-done.16, pred[512,512]{1,0:T(8,128)(4,1)S(1)} %copy-done.13), kind=kOutput, calls=%fused_computation.6.clone.1 | convolution fusion | flops 830472192 | bytes 6078464 | tf_op jit(solution)/shard_map/while/body/eval_jaxpr/hts,shp->thp/dot_general | solution.py:114
  190.4 3.7 %copy.69 = f32[512,1536]{1,0:T(8,128)} copy(f32[512,1536]{0,1:T(8,128)} %bitcast.241) | data formatting | bytes 6291456 | tf_op jit(solution)/shard_map/while/body/eval_jaxpr/reshape | solution.py:116
  194.1 4.3 %fusion.146 = bf16[2,512,1536]{2,1,0:T(8,128)(2,1)} fusion(bf16[2,512,1536]{2,1,0:T(8,128)(2,1)} %get-tuple-element.1064, s32[]{:T(128)S(6)} %copy.117, f32[512,1536]{1,0:T(8,128)} %copy.69, f32[1,512,1536]{2,1,0:T(8,128)S(1)} %copy-done, f32[1536]{0:T(1024)S(1)} %mul.282, bf16[2,128,1536]{2,1,0:T(8,128)(2,1)} %get-tuple-element.1090, ...), kind=kOutput, calls=%fused_computation.28.clone.1 | convolution fusion | flops 206045184 | bytes 9971200 | tf_op jit(solution)/shard_map/while/body/eval_jaxpr/dot_general | solution.py:119
  200.0 2.2 fusion.144
  202.2 2.2 constant_dynamic-slice_fusion.10
  204.4 2.4 copy.70
  206.7 2.1 constant_dynamic-slice_fusion.9
  210.4 1.6 copy.71
  212.0 9.2 %multiply_reduce_fusion.2 = f32[512,512]{1,0:T(8,128)S(1)} fusion(f32[24,512]{1,0:T(8,128)} %dynamic-slice_bitcast_fusion.2, pred[512,512]{1,0:T(8,128)(4,1)} %iota_compare_fusion.2, bf16[512,24,64]{0,2,1:T(8,128)(2,1)} %bitcast.246, bf16[512,24,64]{0,2,1:T(8,128)(2,1)S(1)} %bitcast.244), kind=kOutput, calls=%fused_computation.2.clone.1 | convolution fusion | flops 830210048 | bytes 4505600 | tf_op jit(solution)/shard_map/while/body/eval_jaxpr/thp,shp->hts/dot_general | solution.py:130
  221.2 1.7 fusion.151
  226.0 7.8 %fusion.147 = f32[24,64,512]{2,1,0:T(8,128)} fusion(bf16[512,24,64]{0,2,1:T(8,128)(2,1)S(1)} %bitcast.247, f32[512,512]{1,0:T(8,128)S(1)} %copy-done.7, f32[24,512]{1,0:T(8,128)S(1)} %copy-done.15, pred[512,512]{1,0:T(8,128)(4,1)S(1)} %copy-done.12), kind=kOutput, calls=%fused_computation.5.clone.1 | convolution fusion | flops 830472192 | bytes 6078464 | tf_op jit(solution)/shard_map/while/body/eval_jaxpr/hts,thp->shp/dot_general | solution.py:122
  233.8 2.4 copy.72
  236.2 4.5 %fusion.148 = bf16[2,512,1536]{2,1,0:T(8,128)(2,1)} fusion(bf16[2,512,1536]{2,1,0:T(8,128)(2,1)} %get-tuple-element.1065, s32[]{:T(128)S(6)} %copy.117, f32[512,1536]{1,0:T(8,128)S(1)} %copy.72, f32[2,512,1536]{2,1,0:T(8,128)} %get-tuple-element.1094, f32[1536]{0:T(1024)S(1)} %mul.282, bf16[2,128,1536]{2,1,0:T(8,128)(2,1)} %get-tuple-element.1093, ...), kind=kOutput, calls=%fused_computation.30.clone.1 | convolution fusion | flops 206045184 | bytes 9969152 | tf_op jit(solution)/shard_map/while/body/eval_jaxpr/dot_general | solution.py:127
  240.8 8.3 %fusion.145 = f32[24,64,512]{2,1,0:T(8,128)} fusion(bf16[512,24,64]{0,2,1:T(8,128)(2,1)S(1)} %bitcast.245, f32[512,512]{1,0:T(8,128)S(1)} %copy-done.8, f32[24,512]{1,0:T(8,128)S(1)} %copy-done.16, pred[512,512]{1,0:T(8,128)(4,1)S(1)} %copy-done.13), kind=kOutput, calls=%fused_computation.6.clone.1 | convolution fusion | flops 830472192 | bytes 6078464 | tf_op jit(solution)/shard_map/while/body/eval_jaxpr/hts,shp->thp/dot_general | solution.py:114
  249.1 3.7 %copy.69 = f32[512,1536]{1,0:T(8,128)} copy(f32[512,1536]{0,1:T(8,128)} %bitcast.241) | data formatting | bytes 6291456 | tf_op jit(solution)/shard_map/while/body/eval_jaxpr/reshape | solution.py:116
  252.8 4.3 %fusion.146 = bf16[2,512,1536]{2,1,0:T(8,128)(2,1)} fusion(bf16[2,512,1536]{2,1,0:T(8,128)(2,1)} %get-tuple-element.1064, s32[]{:T(128)S(6)} %copy.117, f32[512,1536]{1,0:T(8,128)} %copy.69, f32[1,512,1536]{2,1,0:T(8,128)S(1)} %copy-done, f32[1536]{0:T(1024)S(1)} %mul.282, bf16[2,128,1536]{2,1,0:T(8,128)(2,1)} %get-tuple-element.1090, ...), kind=kOutput, calls=%fused_computation.28.clone.1 | convolution fusion | flops 206045184 | bytes 9971200 | tf_op jit(solution)/shard_map/while/body/eval_jaxpr/dot_general | solution.py:119
  257.7 19.2 %reduce-scatter.5.cloned.1.call-done = bf16[256,128]{1,0:T(8,128)(2,1)} async-done(((bf16[1024,128]{1,0:T(8,128)(2,1)}), bf16[256,128]{1,0:T(8,128)(2,1)}) %reduce-scatter.5.cloned.1.call-update) | async-done | bytes 65552 | tf_op jit(solution)/shard_map/reduce_scatter | solution.py:169
  276.9 20.7 %reduce-scatter.3.cloned.1.call-done = bf16[256,128]{1,0:T(8,128)(2,1)} async-done(((bf16[1024,128]{1,0:T(8,128)(2,1)}), bf16[256,128]{1,0:T(8,128)(2,1)}) %reduce-scatter.3.cloned.1.call-update) | async-done | bytes 65552 | tf_op jit(solution)/shard_map/reduce_scatter | solution.py:163
  (224 shorter events, 57.2 us)
Async XLA Ops:
  7.2 92.5 %all-gather.8.cloned.1.call-start = ((), (), s32[]{:S(2)}) async-start(), calls=%async_computation.5 | async-start | bytes 3538944 | tf_op jit(solution)/shard_map/all_gather | solution.py:14
  11.2 20.7 %copy-start.17 = (f32[2,512,24]{1,2,0:T(8,128)}, f32[2,512,24]{1,2,0:T(8,128)S(1)}, u32[]{:S(2)}) copy-start(f32[2,512,24]{1,2,0:T(8,128)S(1)} %get-tuple-element.719) | copy-start | bytes 294916
  34.4 3.6 %copy-start.9 = (bf16[2,512,1536]{1,2,0:T(8,128)(2,1)}, bf16[2,512,1536]{1,2,0:T(8,128)(2,1)S(1)}, u32[]{:S(2)}) copy-start(bf16[2,512,1536]{1,2,0:T(8,128)(2,1)S(1)} %multiply_convert_fusion.3) | copy-start | bytes 9437188
  44.3 74.9 %all-gather.6.cloned.1.call-start = ((), (), s32[]{:S(2)}) async-start(), calls=%async_computation.4 | async-start | bytes 3538944 | tf_op jit(solution)/shard_map/all_gather | solution.py:14
  47.8 6.6 %copy-start.21 = (bf16[256,128]{1,0:T(8,128)(2,1)S(1)}, bf16[256,128]{1,0:T(8,128)(2,1)}, u32[]{:S(2)}) copy-start(bf16[256,128]{1,0:T(8,128)(2,1)} %param.17) | copy-start | bytes 196612
  74.4 5.0 %copy-start.1 = (bf16[2,512,1536]{2,1,0:T(8,128)(2,1)}, bf16[2,512,1536]{2,1,0:T(8,128)(2,1)S(1)}, u32[]{:S(2)}) copy-start(bf16[2,512,1536]{2,1,0:T(8,128)(2,1)S(1)} %multiply_convert_fusion.4) | copy-start | bytes 9437188
  79.3 6.4 %copy-start.23 = (u32[32]{0:T(128)S(1)}, u32[32]{0:T(128)}, u32[]{:S(2)}) copy-start(u32[32]{0:T(128)} %constant.164) | copy-start | bytes 388
  85.6 191.3 %reduce-scatter.5.cloned.1.call-start = ((), (), s32[]{:S(2)}) async-start(), calls=%async_computation.3 | async-start | bytes 327680 | tf_op jit(solution)/shard_map/reduce_scatter | solution.py:169
  132.6 2.6 copy-start.14
  132.6 3.8 %copy-start.18 = (f32[2,512,24]{1,2,0:T(8,128)S(1)}, f32[2,512,24]{1,2,0:T(8,128)}, u32[]{:S(2)}) copy-start(f32[2,512,24]{1,2,0:T(8,128)} %copy-done.17) | copy-start | bytes 294916
  136.4 3.4 %copy-start.22 = (f32[24]{0:T(128)S(1)}, f32[24]{0:T(128)}, u32[]{:S(2)}) copy-start(f32[24]{0:T(128)} %param.20) | copy-start | bytes 292
  151.8 1.6 copy-start.3
  153.4 11.9 %copy-start.2 = (bf16[2,512,1536]{2,1,0:T(8,128)(2,1)S(1)}, bf16[2,512,1536]{2,1,0:T(8,128)(2,1)}, u32[]{:S(2)}) copy-start(bf16[2,512,1536]{2,1,0:T(8,128)(2,1)} %get-tuple-element.1095) | copy-start | bytes 9437188 | tf_op jit(solution)/shard_map/while
  153.4 11.9 %copy-start.19 = (bf16[2,512,128]{2,1,0:T(8,128)(2,1)S(1)}, bf16[2,512,128]{2,1,0:T(8,128)(2,1)}, u32[]{:S(2)}) copy-start(bf16[2,512,128]{2,1,0:T(8,128)(2,1)} %get-tuple-element.1066) | copy-start | bytes 786436 | tf_op jit(solution)/shard_map/while
  162.6 2.8 copy-start.6
  162.6 3.4 %copy-start.10 = (bf16[2,512,1536]{1,2,0:T(8,128)(2,1)S(1)}, bf16[2,512,1536]{1,2,0:T(8,128)(2,1)}, u32[]{:S(2)}) copy-start(bf16[2,512,1536]{1,2,0:T(8,128)(2,1)} %get-tuple-element.1096) | copy-start | bytes 9437188 | tf_op jit(solution)/shard_map/while
  162.6 3.4 %copy-start.11 = (bf16[2,128,1536]{2,1,0:T(8,128)(2,1)S(1)}, bf16[2,128,1536]{2,1,0:T(8,128)(2,1)}, u32[]{:S(2)}) copy-start(bf16[2,128,1536]{2,1,0:T(8,128)(2,1)} %get-tuple-element.1090) | copy-start | bytes 2359300 | tf_op jit(solution)/shard_map/while
  164.3 3.0 copy-start.5
  164.3 3.0 copy-start.7
  164.3 3.0 copy-start.12
  164.3 3.0 copy-start.15
  166.0 9.1 %copy-start.20 = (bf16[2,512,128]{2,1,0:T(8,128)(2,1)}, bf16[2,512,128]{2,1,0:T(8,128)(2,1)S(1)}, u32[]{:S(2)}) copy-start(bf16[2,512,128]{2,1,0:T(8,128)(2,1)S(1)} %fusion.150) | copy-start | bytes 786436 | tf_op jit(solution)/shard_map/while
  177.5 4.6 %copy-start.4 = (bf16[1,512,1536]{1,2,0:T(8,128)(2,1)S(1)}, bf16[1,512,1536]{1,2,0:T(8,128)(2,1)}, u32[]{:S(2)}) copy-start(bf16[1,512,1536]{1,2,0:T(8,128)(2,1)} %copy.68) | copy-start | bytes 4718596 | tf_op jit(solution)/shard_map/while
  177.5 4.6 %copy-start.8 = (f32[512,512]{1,0:T(8,128)S(1)}, f32[512,512]{1,0:T(8,128)}, u32[]{:S(2)}) copy-start(f32[512,512]{1,0:T(8,128)} %fusion.144) | copy-start | bytes 3145732 | tf_op jit(solution)/shard_map/while
  177.6 4.6 %copy-start.13 = (pred[512,512]{1,0:T(8,128)(4,1)S(1)}, pred[512,512]{1,0:T(8,128)(4,1)}, u32[]{:S(2)}) copy-start(pred[512,512]{1,0:T(8,128)(4,1)} %iota_compare_fusion.2) | copy-start | bytes 786436 | tf_op jit(solution)/shard_map/while
  177.6 4.6 %copy-start.16 = (f32[24,512]{1,0:T(8,128)S(1)}, f32[24,512]{1,0:T(8,128)}, u32[]{:S(2)}) copy-start(f32[24,512]{1,0:T(8,128)} %dynamic-slice_bitcast_fusion.2) | copy-start | bytes 147460 | tf_op jit(solution)/shard_map/while
  190.4 3.7 %copy-start = (f32[1,512,1536]{2,1,0:T(8,128)S(1)}, f32[1,512,1536]{2,1,0:T(8,128)}, u32[]{:S(2)}) copy-start(f32[1,512,1536]{2,1,0:T(8,128)} %copy.70) | copy-start | bytes 9437188 | tf_op jit(solution)/shard_map/while
  210.4 1.6 copy-start.3
  212.0 11.9 %copy-start.2 = (bf16[2,512,1536]{2,1,0:T(8,128)(2,1)S(1)}, bf16[2,512,1536]{2,1,0:T(8,128)(2,1)}, u32[]{:S(2)}) copy-start(bf16[2,512,1536]{2,1,0:T(8,128)(2,1)} %get-tuple-element.1095) | copy-start | bytes 9437188 | tf_op jit(solution)/shard_map/while
  212.0 11.9 %copy-start.19 = (bf16[2,512,128]{2,1,0:T(8,128)(2,1)S(1)}, bf16[2,512,128]{2,1,0:T(8,128)(2,1)}, u32[]{:S(2)}) copy-start(bf16[2,512,128]{2,1,0:T(8,128)(2,1)} %get-tuple-element.1066) | copy-start | bytes 786436 | tf_op jit(solution)/shard_map/while
  221.2 2.8 copy-start.6
  221.2 3.4 %copy-start.10 = (bf16[2,512,1536]{1,2,0:T(8,128)(2,1)S(1)}, bf16[2,512,1536]{1,2,0:T(8,128)(2,1)}, u32[]{:S(2)}) copy-start(bf16[2,512,1536]{1,2,0:T(8,128)(2,1)} %get-tuple-element.1096) | copy-start | bytes 9437188 | tf_op jit(solution)/shard_map/while
  221.2 3.4 %copy-start.11 = (bf16[2,128,1536]{2,1,0:T(8,128)(2,1)S(1)}, bf16[2,128,1536]{2,1,0:T(8,128)(2,1)}, u32[]{:S(2)}) copy-start(bf16[2,128,1536]{2,1,0:T(8,128)(2,1)} %get-tuple-element.1090) | copy-start | bytes 2359300 | tf_op jit(solution)/shard_map/while
  222.9 3.0 copy-start.5
  222.9 3.0 copy-start.7
  222.9 3.0 copy-start.12
  222.9 3.0 copy-start.15
  224.7 9.1 %copy-start.20 = (bf16[2,512,128]{2,1,0:T(8,128)(2,1)}, bf16[2,512,128]{2,1,0:T(8,128)(2,1)S(1)}, u32[]{:S(2)}) copy-start(bf16[2,512,128]{2,1,0:T(8,128)(2,1)S(1)} %fusion.150) | copy-start | bytes 786436 | tf_op jit(solution)/shard_map/while
  236.2 4.6 %copy-start.4 = (bf16[1,512,1536]{1,2,0:T(8,128)(2,1)S(1)}, bf16[1,512,1536]{1,2,0:T(8,128)(2,1)}, u32[]{:S(2)}) copy-start(bf16[1,512,1536]{1,2,0:T(8,128)(2,1)} %copy.68) | copy-start | bytes 4718596 | tf_op jit(solution)/shard_map/while
  236.2 4.6 %copy-start.8 = (f32[512,512]{1,0:T(8,128)S(1)}, f32[512,512]{1,0:T(8,128)}, u32[]{:S(2)}) copy-start(f32[512,512]{1,0:T(8,128)} %fusion.144) | copy-start | bytes 3145732 | tf_op jit(solution)/shard_map/while
  236.2 4.6 %copy-start.13 = (pred[512,512]{1,0:T(8,128)(4,1)S(1)}, pred[512,512]{1,0:T(8,128)(4,1)}, u32[]{:S(2)}) copy-start(pred[512,512]{1,0:T(8,128)(4,1)} %iota_compare_fusion.2) | copy-start | bytes 786436 | tf_op jit(solution)/shard_map/while
  236.2 4.6 %copy-start.16 = (f32[24,512]{1,0:T(8,128)S(1)}, f32[24,512]{1,0:T(8,128)}, u32[]{:S(2)}) copy-start(f32[24,512]{1,0:T(8,128)} %dynamic-slice_bitcast_fusion.2) | copy-start | bytes 147460 | tf_op jit(solution)/shard_map/while
  249.1 3.7 %copy-start = (f32[1,512,1536]{2,1,0:T(8,128)S(1)}, f32[1,512,1536]{2,1,0:T(8,128)}, u32[]{:S(2)}) copy-start(f32[1,512,1536]{2,1,0:T(8,128)} %copy.70) | copy-start | bytes 9437188 | tf_op jit(solution)/shard_map/while
  257.1 40.5 %reduce-scatter.3.cloned.1.call-start = ((), (), s32[]{:S(2)}) async-start(), calls=%async_computation.2 | async-start | bytes 327680 | tf_op jit(solution)/shard_map/reduce_scatter | solution.py:163
Sparse Core Ops, SparseCore 0:
  44.4 33.8 all-gather.7
  85.7 33.4 all-gather.5
  257.2 19.6 reduce-scatter.4
  279.7 17.9 reduce-scatter.2
where the time goes:
time: 306 us; the launch traced here: 304 us
  matrix products  87.6 us (29%)
  local copies, waits for them, and re-layouts  65.3 us (21%)
  waiting for transfers between devices  46.6 us (15%)
  other arithmetic  46 us (15%)
  blocking collectives  42.9 us (14%)
  between operations  14.7 us (5%)
    select_n x16, other arithmetic, step(): return jax.tree.map(lambda a, b: jnp.where(reached, a, b), new, before)  23.9 us
    reduce_scatter x1, waiting for transfers between devices, local(): lax.psum_scatter(key_grads.reshape(tok_count, STATE).astype(jnp.bfloat16)...  20.7 us
    dynamic_slice x10, local copies, waits for them, and re-layouts, local(): lax.map(one_block, (running, input_blocks, grad_blocks, key_blocks, query...  19.7 us
    reduce_scatter x1, waiting for transfers between devices, local(): lax.psum_scatter(query_grads.reshape(tok_count, STATE).astype(jnp.bfloat1...  19.2 us
    dot_general x2, matrix products, one_block(): jnp.einsum('thp,shp->hts', grad_heads, input_heads, preferred_element_typ...  18.3 us
    dot_general x2, matrix products, one_block(): jnp.einsum('hts,shp->thp', weights, input_heads, preferred_element_type=j...  16.6 us
    all_gather x1, blocking collectives, local(): lax.all_gather(read_queries, 'tp', axis=0, tiled=True)  15.8 us
    dot_general x2, matrix products, one_block(): jnp.einsum('hts,thp->shp', weights, grad_heads, preferred_element_type=jn...  15.7 us
  transfers between devices with their start and end apart: 4, of which 3 were waited for; matrix products, arithmetic and copies ran while one was open for 13% of the time, Pallas kernels for 0%

commit v1 on v0

v1 whole, which is shorter than its diff:
```python
import functools
import jax
import jax.numpy as jnp
import numpy as np
from jax import lax
from jax.experimental import pallas as pl
from jax.experimental.pallas import tpu as pltpu
from jax.sharding import PartitionSpec as P

HEADDIM = 64
CHUNK = 128
HALF = CHUNK // 2
PIECES = 4
MESH = pl.DeviceIdType.MESH
F32 = jnp.float32
BF16 = jnp.bfloat16
LIMIT = 56 * 1024 * 1024
NT = (((1,), (1,)), ((), ()))
TN = (((0,), (0,)), ((), ()))


def exact_nt(a, b):
    return lax.dot_general(a, b, NT, precision=lax.Precision.HIGHEST, preferred_element_type=F32)


def widen(values, spread, heads):
    high = values.astype(BF16)
    low = (values - high.astype(F32)).astype(BF16)
    lane = lax.broadcasted_iota(jnp.int32, values.shape, 1)
    both = jnp.where(lane < heads, high.astype(F32), low.astype(F32)).astype(BF16)
    return jnp.dot(both, spread, preferred_element_type=F32)


def about_middle():
    row = lax.broadcasted_iota(jnp.int32, (CHUNK + 8, CHUNK), 0)
    col = lax.broadcasted_iota(jnp.int32, (CHUNK + 8, CHUNK), 1)
    first = jnp.where(col < HALF, 1.0, 0.0)
    inner = jnp.where(col <= row, 1.0, 0.0) - first
    tail = jnp.where(row == CHUNK, first, jnp.where(row == CHUNK + 1, 1.0 - first, 0.0))
    return jnp.where(row < CHUNK, inner, tail)


def gather_kernel(
    nseq, ntp, heads,
    x_ref, g_ref, k_ref, q_ref, ld_ref, e_ref,
    xs_ref, gs_ref, kout_ref, qout_ref, sin_ref, cin_ref,
    kbuf, qbuf, tsum, csum, factors, srecv, crecv, ssend, csend,
    ag_send, ag_recv, st_send, st_recv, ct_send, ct_recv,
):
    seq, tp = lax.axis_index("seq"), lax.axis_index("tp")
    rows = k_ref.shape[0]
    chunks = x_ref.shape[0] // CHUNK
    per = rows // CHUNK
    right, left = lax.rem(seq + 1, nseq), lax.rem(seq + nseq - 1, nseq)

    barrier = pltpu.get_barrier_semaphore()
    for k in range(1, ntp):
        pl.semaphore_signal(
            barrier, inc=1, device_id={"tp": lax.rem(tp + k, ntp)}, device_id_type=MESH
        )
    for other in (left, right):
        pl.semaphore_signal(barrier, inc=1, device_id={"seq": other}, device_id_type=MESH)
    pl.semaphore_wait(barrier, ntp - 1 + 2)

    def ag_copy(which, k, place):
        src, dst = ((k_ref, kbuf), (q_ref, qbuf))[which]
        return pltpu.make_async_remote_copy(
            src_ref=src,
            dst_ref=dst.at[pl.ds(pl.multiple_of(place * rows, rows), rows)],
            send_sem=ag_send.at[which, k],
            recv_sem=ag_recv.at[which, k],
            device_id={"tp": lax.rem(tp + k, ntp)},
            device_id_type=MESH,
        )

    for k in range(ntp - 1, 0, -1):
        for which in range(2):
            ag_copy(which, k, tp).start()

    own = pl.ds(pl.multiple_of(tp * rows, rows), rows)
    kbuf[own, :] = k_ref[...]
    qbuf[own, :] = q_ref[...]

    spread = e_ref[...]
    tokens = x_ref.shape[0]
    row = lax.broadcasted_iota(jnp.int32, (chunks, tokens), 0)
    col = lax.broadcasted_iota(jnp.int32, (chunks, tokens), 1)
    before = jnp.where(col < row * CHUNK + HALF, 1.0, 0.0)
    logs = ld_ref[...]
    sums = jnp.concatenate(
        [
            exact_nt(1.0 - before, logs),
            exact_nt(before, logs),
            exact_nt(jnp.ones((chunks, tokens), F32), logs),
        ],
        axis=0,
    )
    factors[...] = widen(jnp.exp(sums), spread, heads)

    def scale(c, carry):
        at = pl.ds(pl.multiple_of(c * CHUNK, CHUNK), CHUNK)
        d = exact_nt(about_middle()[:CHUNK], ld_ref[:, at])
        a = widen(jnp.exp(-d), spread, heads)
        xs_ref[at, :] = (x_ref[at, :].astype(F32) * a).astype(BF16)
        b = widen(jnp.exp(d), spread, heads)
        gs_ref[at, :] = (g_ref[at, :].astype(F32) * b).astype(BF16)
        return carry

    lax.fori_loop(0, chunks, scale, 0)

    tsum[...] = jnp.zeros_like(tsum)
    csum[...] = jnp.zeros_like(csum)

    def add_chunk(c):
        at = pl.ds(pl.multiple_of(c * CHUNK, CHUNK), CHUNK)
        up = lax.dot_general(kbuf[at, :], xs_ref[at, :], TN, preferred_element_type=F32)
        tsum[...] += factors[pl.ds(c, 1), :] * up
        down = lax.dot_general(qbuf[at, :], gs_ref[at, :], TN, preferred_element_type=F32)
        csum[...] += factors[pl.ds(chunks + c, 1), :] * down

    for k in range(ntp):
        place = lax.rem(tp - k + ntp, ntp)
        if k > 0:
            for which in range(2):
                ag_copy(which, k, place).wait_recv()

        def one(j, carry, place=place):
            add_chunk(place * per + j)
            return carry

        lax.fori_loop(0, per, one, 0)

    whole = factors[2 * chunks : 2 * chunks + 1, :]
    step = tsum.shape[0] // PIECES

    def chain(own_sum, got, out, send, recv, first, last, nxt):
        @pl.when(seq == first)
        def _():
            got[...] = jnp.zeros_like(got)

        def piece(p, carry):
            at = pl.ds(pl.multiple_of(p * step, step), step)
            copy = pltpu.make_async_remote_copy(
                src_ref=out.at[at],
                dst_ref=got.at[at],
                send_sem=send.at[p],
                recv_sem=recv.at[p],
                device_id={"seq": nxt},
                device_id_type=MESH,
            )

            @pl.when(seq != first)
            def _():
                copy.wait_recv()

            @pl.when(seq != last)
            def _():
                out[at, :] = (whole * got[at, :].astype(F32) + own_sum[at, :]).astype(BF16)
                copy.start()

            return carry

        lax.fori_loop(0, PIECES, piece, 0)

    def states():
        chain(tsum, srecv, ssend, st_send, st_recv, 0, nseq - 1, right)

    def cotangents():
        chain(csum, crecv, csend, ct_send, ct_recv, nseq - 1, 0, left)

    early = 2 * seq < nseq

    @pl.when(early)
    def _():
        states()
        cotangents()

    @pl.when(jnp.logical_not(early))
    def _():
        cotangents()
        states()

    kout_ref[...] = kbuf[...]
    qout_ref[...] = qbuf[...]
    sin_ref[...] = srecv[...]
    cin_ref[...] = crecv[...]

    def drain(out, got, send, recv, nxt, last):
        @pl.when(seq != last)
        def _():
            for p in range(PIECES):
                at = pl.ds(p * step, step)
                pltpu.make_async_remote_copy(
                    src_ref=out.at[at], dst_ref=got.at[at], send_sem=send.at[p], recv_sem=recv.at[p],
                    device_id={"seq": nxt}, device_id_type=MESH,
                ).wait_send()

    drain(ssend, srecv, st_send, st_recv, right, nseq - 1)
    drain(csend, crecv, ct_send, ct_recv, left, 0)
    for k in range(1, ntp):
        for which in range(2):
            ag_copy(which, k, tp).wait_send()


def main_kernel(
    heads,
    xf, gf, kf, qf, xb, gb, kb, qb, ld_ref, e_ref, skip_ref, s_in, c_in,
    mixed_ref, grad_ref, read_ref, write_ref,
    state, cot, fstack, bstack,
):
    i = pl.program_id(0)
    n = pl.num_programs(0)
    j = n - 1 - i

    @pl.when(i == 0)
    def _():
        state[...] = s_in[...].astype(F32)
        cot[...] = c_in[...].astype(F32)

    spread = e_ref[...]
    middle = about_middle()
    skip = widen(jnp.broadcast_to(skip_ref[...], (8, skip_ref.shape[1])), spread, heads)[0:1, :]
    row = lax.broadcasted_iota(jnp.int32, (CHUNK, CHUNK), 0)
    col = lax.broadcasted_iota(jnp.int32, (CHUNK, CHUNK), 1)
    lower, upper = row >= col, row <= col

    def one(c, flip, left, keys, x, g, stack, carry):
        at = pl.ds(pl.multiple_of(c * CHUNK, CHUNK), CHUNK)
        d = exact_nt(middle, ld_ref[:, at])
        srow = lax.broadcasted_iota(jnp.int32, d.shape, 0)
        if flip:
            d = jnp.where(srow < CHUNK, -d, d)
        factor = widen(jnp.exp(d), spread, heads)
        outer = factor[:CHUNK]
        first, second = factor[CHUNK : CHUNK + 1], factor[CHUNK + 1 : CHUNK + 2]
        if flip:
            first, second = second, first
        mask = upper if flip else lower
        gram = lax.dot_general(left, keys, NT, preferred_element_type=F32)
        gram = jnp.where(mask, gram, 0.0).astype(BF16)
        low = first * carry[...]
        stack[0:CHUNK, :] = x
        stack[CHUNK:, :] = low.astype(BF16)
        total = jnp.dot(
            jnp.concatenate([gram, left], axis=1), stack[...], preferred_element_type=F32
        )
        out = (outer * (total + skip * x.astype(F32))).astype(BF16)
        both = lax.dot_general(g, stack[...], NT, preferred_element_type=F32)
        mixer = jnp.where(mask, both[:, :CHUNK], 0.0).astype(BF16)
        small = jnp.dot(mixer, keys, preferred_element_type=F32) + both[:, CHUNK:]
        carry[...] = second * (low + lax.dot_general(keys, x, TN, preferred_element_type=F32))
        return out, small.astype(BF16)

    mixed_ref[...], read_ref[...] = one(
        i, False, qf[...], kf[...], xf[...], gf[...], fstack, state
    )
    grad_ref[...], write_ref[...] = one(
        j, True, kb[...], qb[...], gb[...], xb[...], bstack, cot
    )


def scatter_kernel(ntp, w_ref, r_ref, wout, rout, got, send, recv):
    tp = lax.axis_index("tp")
    rows = wout.shape[0]
    barrier = pltpu.get_barrier_semaphore()
    for k in range(1, ntp):
        pl.semaphore_signal(
            barrier, inc=1, device_id={"tp": lax.rem(tp + k, ntp)}, device_id_type=MESH
        )
    pl.semaphore_wait(barrier, ntp - 1)

    def copy(which, k):
        src = (w_ref, r_ref)[which]
        peer = lax.rem(tp + k, ntp)
        return pltpu.make_async_remote_copy(
            src_ref=src.at[pl.ds(pl.multiple_of(peer * rows, rows), rows)],
            dst_ref=got.at[which, k - 1],
            send_sem=send.at[which, k],
            recv_sem=recv.at[which, k],
            device_id={"tp": peer},
            device_id_type=MESH,
        )

    for k in range(ntp - 1, 0, -1):
        for which in range(2):
            copy(which, k).start()
    own = pl.ds(pl.multiple_of(tp * rows, rows), rows)
    for which, (src, out) in enumerate(((w_ref, wout), (r_ref, rout))):
        total = src[own, :].astype(F32)
        for k in range(1, ntp):
            copy(which, k).wait_recv()
            total = total + got[which, k - 1].astype(F32)
        out[...] = total.astype(BF16)
    for k in range(1, ntp):
        for which in range(2):
            copy(which, k).wait_send()


def local(nseq, ntp, head_inputs, write_keys, read_queries, log_decay, skip_gain, out_grad):
    tokens, width = head_inputs.shape
    heads = width // HEADDIM
    rows, size = write_keys.shape
    chunks = tokens // CHUNK
    place = np.arange(2 * heads)[:, None] % heads == np.arange(width)[None, :] // HEADDIM
    spread = jnp.asarray(place.astype(np.float32), BF16)
    logs = jnp.concatenate([log_decay, log_decay], axis=0)
    skip = jnp.concatenate([skip_gain, skip_gain])[None, :]
    vmem = pl.BlockSpec(memory_space=pltpu.VMEM)
    dma = pltpu.SemaphoreType.DMA
    big = jax.ShapeDtypeStruct((tokens, width), BF16)
    small = jax.ShapeDtypeStruct((tokens, size), BF16)
    edge = jax.ShapeDtypeStruct((size, width), BF16)
    xs, gs, keys, queries, s_in, c_in = pl.pallas_call(
        functools.partial(gather_kernel, nseq, ntp, heads),
        out_shape=(big, big, small, small, edge, edge),
        in_specs=[vmem] * 6,
        out_specs=[vmem] * 6,
        scratch_shapes=[
            pltpu.VMEM((tokens, size), BF16),
            pltpu.VMEM((tokens, size), BF16),
            pltpu.VMEM((size, width), F32),
            pltpu.VMEM((size, width), F32),
            pltpu.VMEM((3 * chunks, width), F32),
            pltpu.VMEM((size, width), BF16),
            pltpu.VMEM((size, width), BF16),
            pltpu.VMEM((size, width), BF16),
            pltpu.VMEM((size, width), BF16),
            dma((2, ntp)),
            dma((2, ntp)),
            dma((PIECES,)),
            dma((PIECES,)),
            dma((PIECES,)),
            dma((PIECES,)),
        ],
        compiler_params=pltpu.CompilerParams(
            collective_id=0, has_side_effects=True, vmem_limit_bytes=LIMIT
        ),
        name="gather_states",
    )(head_inputs, out_grad, write_keys, read_queries, logs, spread)

    def fwd(block):
        return pl.BlockSpec(block, lambda i: (i, 0))

    def bwd(block):
        return pl.BlockSpec(block, lambda i: (chunks - 1 - i, 0))

    def full(shape):
        return pl.BlockSpec(shape, lambda i: (0, 0))

    wide, thin = (CHUNK, width), (CHUNK, size)
    mixed, grad, read, write = pl.pallas_call(
        functools.partial(main_kernel, heads),
        grid=(chunks,),
        out_shape=(big, big, small, small),
        in_specs=[fwd(wide), fwd(wide), fwd(thin), fwd(thin)]
        + [bwd(wide), bwd(wide), bwd(thin), bwd(thin)]
        + [full(logs.shape), full(spread.shape), full(skip.shape), full((size, width)), full((size, width))],
        out_specs=[fwd(wide), bwd(wide), fwd(thin), bwd(thin)],
        scratch_shapes=[
            pltpu.VMEM((size, width), F32),
            pltpu.VMEM((size, width), F32),
            pltpu.VMEM((CHUNK + size, width), BF16),
            pltpu.VMEM((CHUNK + size, width), BF16),
        ],
        compiler_params=pltpu.CompilerParams(vmem_limit_bytes=LIMIT),
        name="outputs",
    )(xs, gs, keys, queries, xs, gs, keys, queries, logs, spread, skip, s_in, c_in)

    part = jax.ShapeDtypeStruct((rows, size), BF16)
    write_grad, read_grad = pl.pallas_call(
        functools.partial(scatter_kernel, ntp),
        out_shape=(part, part),
        in_specs=[vmem, vmem],
        out_specs=[vmem, vmem],
        scratch_shapes=[
            pltpu.VMEM((2, ntp - 1, rows, size), BF16),
            dma((2, ntp)),
            dma((2, ntp)),
        ],
        compiler_params=pltpu.CompilerParams(collective_id=1, has_side_effects=True),
        name="scatter_grads",
    )(write, read)
    return mixed, grad, write_grad, read_grad


def solution(mesh):
    in_specs = (
        P("seq", "tp"),
        P(("seq", "tp"), None),
        P(("seq", "tp"), None),
        P("tp", "seq"),
        P("tp"),
        P("seq", "tp"),
    )
    out_specs = (P("seq", "tp"), P("seq", "tp"), P(("seq", "tp"), None), P(("seq", "tp"), None))
    body = functools.partial(local, mesh.shape["seq"], mesh.shape["tp"])
    return jax.shard_map(body, mesh=mesh, in_specs=in_specs, out_specs=out_specs, check_vma=False)
```

time: 306 us -> 93.6 us (0.31)
  matrix products: 87.6 us -> 0 us
  Pallas kernels: 0 us -> 85.9 us
  local copies, waits for them, and re-layouts: 65.3 us -> 5.43 us
  waiting for transfers between devices: 46.6 us -> 0 us
  other arithmetic: 46 us -> 1.32 us
  blocking collectives: 42.9 us -> 0 us
  between operations: 14.7 us -> 0.66 us
    dot_general x22 -> x0, matrix products: 87.6 us -> none  [the longest x2 18.3 us: one_block(): jnp.einsum('thp,shp->hts', grad_heads, input_heads, preferred_element_typ...]
    pallas_call x0 -> x3, Pallas kernels: none -> 85.9 us  [the longest x1 42.6 us: local(): pl.pallas_call(functools.partial(gather_kernel, nseq, ntp, heads), out_sh...]
    reduce_scatter x2 -> x0, waiting for transfers between devices: 40 us -> none  [the longest x1 20.7 us: local(): lax.psum_scatter(key_grads.reshape(tok_count, STATE).astype(jnp.bfloat16)...]
    all_gather x2 -> x0, blocking collectives: 30.9 us -> none  [the longest x1 15.8 us: local(): lax.all_gather(read_queries, 'tp', axis=0, tiled=True)]
    dynamic_slice x22 -> x0, local copies, waits for them, and re-layouts: 25.6 us -> none  [the longest x10 19.7 us: local(): lax.map(one_block, (running, input_blocks, grad_blocks, key_blocks, query...]
    select_n x16 -> x0, other arithmetic: 23.9 us -> none  [step(): return jax.tree.map(lambda a, b: jnp.where(reached, a, b), new, before)]
    reshape x6 -> x0, local copies, waits for them, and re-layouts: 23.4 us -> none  [the longest x2 7.39 us: one_block(): forward_part = jnp.einsum('hts,shp->thp', weights, input_heads, preferred...]
    convert_element_type x7 -> x0, other arithmetic: 12.7 us -> none  [the longest x1 4.8 us: local(): scaled_inputs = (input_blocks * to_end).astype(jnp.bfloat16)]
  transfers between devices with their start and end apart: 4 -> 0, of which waited for: 3 -> 0; matrix products, arithmetic and copies ran while one was open for 13% -> 0% of each run, Pallas kernels for 0% -> 0%
where the time goes in v1:
time: 93.6 us; the launch traced here: 93.3 us
  Pallas kernels  85.9 us (92%)
  local copies, waits for them, and re-layouts  5.43 us (6%)
  other arithmetic  1.32 us (1%)
    pallas_call x1, Pallas kernels, local(): pl.pallas_call(functools.partial(gather_kernel, nseq, ntp, heads), out_sh...  42.6 us
    pallas_call x1, Pallas kernels, local(): pl.pallas_call(functools.partial(main_kernel, heads), grid=(chunks,), out...  26.6 us
    pallas_call x1, Pallas kernels, local(): pl.pallas_call(functools.partial(scatter_kernel, ntp), out_shape=(part, p...  16.6 us
    unnamed x5, local copies, waits for them, and re-layouts  4.53 us

profile of v1, /device:TPU:0, one launch (start us, length us, event | category | flops | bytes accessed | tf_op | source)
XLA Modules:
  0.0 93.3 jit_solution(9573503012593386065)
XLA Ops:
  0.6 1.3 %maximum_bitcast_fusion.skip_ref = f32[1,48]{1,0:T(1,128)} fusion(f32[24]{0:T(128)} %param.11), kind=kLoop, calls=%fused_computation.2 | loop fusion | flops 48 | bytes 288 | tf_op jit(solution)/shard_map/broadcast_in_dim | solution.py:307
  1.9 0.9 constant_dynamic-update-slice_fusion.1
  2.8 0.9 constant_dynamic-update-slice_fusion.ld_ref
  3.7 0.0 copy-start
  3.8 0.7 copy-done
  4.4 42.6 %gather_states.1 = (bf16[1024,1536]{1,0:T(8,128)(2,1)}, bf16[1024,1536]{1,0:T(8,128)(2,1)}, bf16[1024,128]{1,0:T(8,128)(2,1)}, bf16[1024,128]{1,0:T(8,128)(2,1)}...) custom-call(bf16[1024,1536]{1,0:T(8,128)(2,1)} %x_ref.1, bf16[1024,1536]{1,0:T(8,128)(2,1)} %g_ref.1, ...), custom_call_target="tpu_custom_call" | custom-call | tf_op jit(solution)/shard_map/gather_states/pallas_call | solution.py:313
  47.1 26.6 %outputs.1 = (bf16[1024,1536]{1,0:T(8,128)(2,1)}, bf16[1024,1536]{1,0:T(8,128)(2,1)}, bf16[1024,128]{1,0:T(8,128)(2,1)}, bf16[1024,128]{1,0:T(8,128)(2,1)}) custom-call(bf16[1024,1536]{1,0:T(8,128)(2,1)} %get-tuple-element.16.xf.xb, bf16[1024,1536]{1,0:T(8,128)(2,1)} %get-tuple-element.17.gf.gb, bf16[1024,128]{1,0:T(8,128)(2,1)} %get-tuple-element.18.kf.kb, ...), custom_call_target="tpu_custom_call" | custom-call | tf_op jit(solution)/shard_map/outputs/pallas_call | solution.py:351
  73.7 16.6 %scatter_grads.1 = (bf16[256,128]{1,0:T(8,128)(2,1)}, bf16[256,128]{1,0:T(8,128)(2,1)}) custom-call(bf16[1024,128]{1,0:T(8,128)(2,1)} %get-tuple-element.24.w_ref, bf16[1024,128]{1,0:T(8,128)(2,1)} %get-tuple-element.25.r_ref), custom_call_target="tpu_custom_call" | custom-call | tf_op jit(solution)/shard_map/scatter_grads/pallas_call | solution.py:370
  90.3 1.5 %copy.14 = bf16[256,128]{1,0:T(8,128)(2,1)} copy(bf16[256,128]{1,0:T(8,128)(2,1)} %get-tuple-element.34) | data formatting | bytes 131072
  91.8 1.5 %copy.15 = bf16[256,128]{1,0:T(8,128)(2,1)} copy(bf16[256,128]{1,0:T(8,128)(2,1)} %get-tuple-element.35) | data formatting | bytes 131072
Async XLA Ops:
  3.7 0.7 copy-start

commit v2 on v1

v2 whole, which is shorter than its diff:
```python
import functools
import jax
import jax.numpy as jnp
from jax import lax
from jax.experimental import pallas as pl
from jax.experimental.pallas import tpu as pltpu
from jax.sharding import PartitionSpec as P

CHUNK = 128
HALF = CHUNK // 2
LANES = 128
PIECES = 8
MESH = pl.DeviceIdType.MESH
F32 = jnp.float32
BF16 = jnp.bfloat16
LIMIT = 56 * 1024 * 1024
NT = (((1,), (1,)), ((), ()))
TN = (((0,), (0,)), ((), ()))


def exact_nt(a, b):
    return lax.dot_general(a, b, NT, precision=lax.Precision.HIGHEST, preferred_element_type=F32)


def widen(values, width):
    rows, heads = values.shape
    dim = width // heads
    each = LANES // dim
    lane = lax.broadcasted_iota(jnp.int32, (rows, LANES), 1)
    tiles = []
    for p in range(width // LANES):
        tile = jnp.broadcast_to(values[:, p * each : p * each + 1], (rows, LANES))
        for e in range(1, each):
            h = p * each + e
            nxt = jnp.broadcast_to(values[:, h : h + 1], (rows, LANES))
            tile = jnp.where(lane >= e * dim, nxt, tile)
        tiles.append(tile)
    return jnp.concatenate(tiles, axis=1)


def rows_at(c, size):
    return pl.ds(pl.multiple_of(c * size, size), size)


def kernel(
    nseq, ntp,
    x_hbm, g_hbm, k_ref, q_ref, ld_ref, skip_ref,
    mixed_hbm, grad_hbm, wout, rout,
    x_ref, g_ref, xs_ref, gs_ref, xe_ref, ge_ref, kbuf, qbuf, tsum, csum, factors, ea_ref, eb_ref,
    srecv, crecv, ssend, csend, fstack, bstack, wpart, rpart, got,
    load_sem, store_sem, ag_send, ag_recv, st_send, st_recv, ct_send, ct_recv, rs_send, rs_recv,
):
    seq, tp = lax.axis_index("seq"), lax.axis_index("tp")
    rows = k_ref.shape[0]
    tokens, width = x_ref.shape
    chunks = tokens // CHUNK
    per = rows // CHUNK
    right, left = lax.rem(seq + 1, nseq), lax.rem(seq + nseq - 1, nseq)

    def load(which, c):
        src, dst = ((x_hbm, x_ref), (g_hbm, g_ref))[which]
        at = rows_at(c, CHUNK)
        return pltpu.make_async_copy(src.at[at], dst.at[at], load_sem.at[which, c])

    def start_loads(c, carry):
        load(0, c).start()
        load(1, c).start()
        return carry

    lax.fori_loop(0, chunks, start_loads, 0)

    barrier = pltpu.get_barrier_semaphore()
    for k in range(1, ntp):
        pl.semaphore_signal(
            barrier, inc=1, device_id={"tp": lax.rem(tp + k, ntp)}, device_id_type=MESH
        )
    for other in (left, right):
        pl.semaphore_signal(barrier, inc=1, device_id={"seq": other}, device_id_type=MESH)
    pl.semaphore_wait(barrier, ntp - 1 + 2)

    def ag_copy(which, k, place):
        src, dst = ((k_ref, kbuf), (q_ref, qbuf))[which]
        return pltpu.make_async_remote_copy(
            src_ref=src,
            dst_ref=dst.at[rows_at(place, rows)],
            send_sem=ag_send.at[which, k],
            recv_sem=ag_recv.at[which, k],
            device_id={"tp": lax.rem(tp + k, ntp)},
            device_id_type=MESH,
        )

    for k in range(ntp - 1, 0, -1):
        for which in range(2):
            ag_copy(which, k, tp).start()

    own = rows_at(tp, rows)
    kbuf[own, :] = k_ref[...]
    qbuf[own, :] = q_ref[...]

    row = lax.broadcasted_iota(jnp.int32, (chunks, tokens), 0) * CHUNK
    col = lax.broadcasted_iota(jnp.int32, (chunks, tokens), 1)
    before = jnp.where(col < row + HALF, 1.0, 0.0)
    logs = ld_ref[...]
    kinds = (
        1.0 - before,
        before,
        jnp.ones((chunks, tokens), F32),
        jnp.where(col >= row, before, 0.0),
        jnp.where(col < row + CHUNK, 1.0 - before, 0.0),
    )
    for n, kind in enumerate(kinds):
        factors[n * chunks : (n + 1) * chunks, :] = widen(jnp.exp(exact_nt(kind, logs)), width)

    def factor(n, c):
        return factors[pl.ds(n * chunks + c, 1), :]

    trow = lax.broadcasted_iota(jnp.int32, (CHUNK, CHUNK), 0)
    tcol = lax.broadcasted_iota(jnp.int32, (CHUNK, CHUNK), 1)
    lower, upper = trow >= tcol, trow <= tcol
    about_middle = jnp.where(lower, 1.0, 0.0) - jnp.where(tcol < HALF, 1.0, 0.0)

    def scale(c, carry):
        at = rows_at(c, CHUNK)
        d = exact_nt(about_middle, ld_ref[:, at])
        a, b = jnp.exp(-d), jnp.exp(d)
        ea_ref[at, :] = a
        eb_ref[at, :] = b
        load(0, c).wait()
        x = x_ref[at, :].astype(F32) * widen(a, width)
        xs_ref[at, :] = x.astype(BF16)
        xe_ref[at, :] = (x * factor(0, c)).astype(BF16)
        load(1, c).wait()
        g = g_ref[at, :].astype(F32) * widen(b, width)
        gs_ref[at, :] = g.astype(BF16)
        ge_ref[at, :] = (g * factor(1, c)).astype(BF16)
        return carry

    lax.fori_loop(0, chunks, scale, 0)

    for k in range(ntp):
        place = lax.rem(tp - k + ntp, ntp)
        if k > 0:
            for which in range(2):
                ag_copy(which, k, place).wait_recv()
        at = rows_at(place, rows)
        up = lax.dot_general(kbuf[at, :], xe_ref[at, :], TN, preferred_element_type=F32)
        down = lax.dot_general(qbuf[at, :], ge_ref[at, :], TN, preferred_element_type=F32)
        if k == 0:
            tsum[...] = up
            csum[...] = down
        else:
            tsum[...] += up
            csum[...] += down

    whole = factors[2 * chunks : 2 * chunks + 1, :]
    step = tsum.shape[0] // PIECES

    def hop(p, out, got_ref, send, recv, nxt):
        at = rows_at(p, step)
        return at, pltpu.make_async_remote_copy(
            src_ref=out.at[at],
            dst_ref=got_ref.at[at],
            send_sem=send.at[p],
            recv_sem=recv.at[p],
            device_id={"seq": nxt},
            device_id_type=MESH,
        )

    def chain(own_sum, got_ref, out, send, recv, first, last, nxt):
        @pl.when(seq == first)
        def _():
            got_ref[...] = jnp.zeros_like(got_ref)

        def piece(p, carry):
            at, copy = hop(p, out, got_ref, send, recv, nxt)

            @pl.when(seq != first)
            def _():
                copy.wait_recv()

            @pl.when(seq != last)
            def _():
                out[at, :] = (whole * got_ref[at, :].astype(F32) + own_sum[at, :]).astype(BF16)
                copy.start()

            return carry

        lax.fori_loop(0, PIECES, piece, 0)

    def states():
        chain(tsum, srecv, ssend, st_send, st_recv, 0, nseq - 1, right)

    def cotangents():
        chain(csum, crecv, csend, ct_send, ct_recv, nseq - 1, 0, left)

    early = 2 * seq < nseq

    @pl.when(early)
    def _():
        states()
        cotangents()

    @pl.when(jnp.logical_not(early))
    def _():
        cotangents()
        states()

    tsum[...] = srecv[...].astype(F32)
    csum[...] = crecv[...].astype(F32)

    skip = widen(jnp.broadcast_to(skip_ref[...], (8, skip_ref.shape[1])), width)[0:1, :]

    def one(c, flip, left_ref, right_ref, a_ref, b_ref, outer_ref, stack, carry, out, small):
        at = rows_at(c, CHUNK)
        lhs, rhs = left_ref[at, :], right_ref[at, :]
        x = a_ref[at, :]
        first, second = (factor(4, c), factor(3, c)) if flip else (factor(3, c), factor(4, c))
        mask = upper if flip else lower
        gram = lax.dot_general(lhs, rhs, NT, preferred_element_type=F32)
        gram = jnp.where(mask, gram, 0.0).astype(BF16)
        low = first * carry[...]
        stack[0:CHUNK, :] = x
        stack[CHUNK:, :] = low.astype(BF16)
        turned = rhs.astype(F32).T.astype(BF16)
        both = jnp.concatenate(
            [
                jnp.concatenate([gram, lhs], axis=1),
                jnp.concatenate([turned, jnp.zeros((turned.shape[0], lhs.shape[1]), BF16)], axis=1),
            ],
            axis=0,
        )
        result = jnp.dot(both, stack[...], preferred_element_type=F32)
        outer = widen(outer_ref[at, :], width)
        out[at, :] = (outer * (result[:CHUNK] + skip * x.astype(F32))).astype(BF16)
        carry[...] = second * (low + result[CHUNK:])
        pair = lax.dot_general(b_ref[at, :], stack[...], NT, preferred_element_type=F32)
        mixer = jnp.where(mask, pair[:, :CHUNK], 0.0).astype(BF16)
        small[at, :] = (
            jnp.dot(mixer, rhs, preferred_element_type=F32) + pair[:, CHUNK:]
        ).astype(BF16)

    def store(which, c):
        src, dst = ((xe_ref, mixed_hbm), (ge_ref, grad_hbm))[which]
        at = rows_at(c, CHUNK)
        return pltpu.make_async_copy(src.at[at], dst.at[at], store_sem.at[which, c])

    def rs_copy(which, k, j, c, peer):
        src = (rpart, wpart)[which]
        return pltpu.make_async_remote_copy(
            src_ref=src.at[rows_at(c, CHUNK)],
            dst_ref=got.at[which, k - 1, rows_at(j, CHUNK)],
            send_sem=rs_send.at[which, k - 1, j],
            recv_sem=rs_recv.at[which, k - 1, j],
            device_id={"tp": peer},
            device_id_type=MESH,
        )

    def send_part(which, c):
        peer = c // per
        k = lax.rem(peer - tp + ntp, ntp)

        @pl.when(k != 0)
        def _():
            rs_copy(which, k, c - peer * per, c, peer).start()

    def block(i, carry):
        j = chunks - 1 - i
        one(i, False, qbuf, kbuf, xs_ref, gs_ref, eb_ref, fstack, tsum, xe_ref, rpart)
        one(j, True, kbuf, qbuf, gs_ref, xs_ref, ea_ref, bstack, csum, ge_ref, wpart)
        store(0, i).start()
        store(1, j).start()
        send_part(0, i)
        send_part(1, j)
        return carry

    lax.fori_loop(0, chunks, block, 0)

    for which, (src, out) in enumerate(((rpart, rout), (wpart, wout))):
        total = src[own, :].astype(F32)
        for k in range(1, ntp):
            for j in range(per):
                rs_copy(which, k, j, 0, lax.rem(tp + k, ntp)).wait_recv()
            total = total + got[which, k - 1].astype(F32)
        out[...] = total.astype(BF16)

    for k in range(1, ntp):
        for which in range(2):
            ag_copy(which, k, tp).wait_send()
            for j in range(per):
                peer = lax.rem(tp + k, ntp)
                rs_copy(which, k, j, peer * per + j, peer).wait_send()

    def finish(c, carry):
        store(0, c).wait()
        store(1, c).wait()
        return carry

    lax.fori_loop(0, chunks, finish, 0)

    def drain(out, got_ref, send, recv, nxt, last):
        @pl.when(seq != last)
        def _():
            def one_piece(p, carry):
                hop(p, out, got_ref, send, recv, nxt)[1].wait_send()
                return carry

            lax.fori_loop(0, PIECES, one_piece, 0)

    drain(ssend, srecv, st_send, st_recv, right, nseq - 1)
    drain(csend, crecv, ct_send, ct_recv, left, 0)


def local(nseq, ntp, head_inputs, write_keys, read_queries, log_decay, skip_gain, out_grad):
    tokens, width = head_inputs.shape
    rows, size = write_keys.shape
    heads = log_decay.shape[0]
    chunks = tokens // CHUNK
    vmem = pl.BlockSpec(memory_space=pltpu.VMEM)
    hbm = pl.BlockSpec(memory_space=pl.ANY)
    dma = pltpu.SemaphoreType.DMA
    big = jax.ShapeDtypeStruct((tokens, width), BF16)
    part = jax.ShapeDtypeStruct((rows, size), BF16)
    wide, tall = pltpu.VMEM((tokens, width), BF16), pltpu.VMEM((tokens, size), BF16)
    edge, total = pltpu.VMEM((size, width), BF16), pltpu.VMEM((size, width), F32)
    by_head = pltpu.VMEM((tokens, heads), F32)
    stack = pltpu.VMEM((CHUNK + size, width), BF16)
    return pl.pallas_call(
        functools.partial(kernel, nseq, ntp),
        out_shape=(big, big, part, part),
        in_specs=[hbm, hbm, vmem, vmem, vmem, vmem],
        out_specs=[hbm, hbm, vmem, vmem],
        scratch_shapes=[wide] * 6
        + [tall, tall, total, total, pltpu.VMEM((5 * chunks, width), F32), by_head, by_head]
        + [edge] * 4
        + [stack, stack, tall, tall, pltpu.VMEM((2, ntp - 1, rows, size), BF16)]
        + [dma((2, chunks)), dma((2, chunks)), dma((2, ntp)), dma((2, ntp))]
        + [dma((PIECES,))] * 4
        + [dma((2, ntp - 1, rows // CHUNK))] * 2,
        compiler_params=pltpu.CompilerParams(
            collective_id=0, has_side_effects=True, vmem_limit_bytes=LIMIT
        ),
        name="ssd_layer",
    )(head_inputs, out_grad, write_keys, read_queries, log_decay, skip_gain[None, :])


def solution(mesh):
    in_specs = (
        P("seq", "tp"),
        P(("seq", "tp"), None),
        P(("seq", "tp"), None),
        P("tp", "seq"),
        P("tp"),
        P("seq", "tp"),
    )
    out_specs = (P("seq", "tp"), P("seq", "tp"), P(("seq", "tp"), None), P(("seq", "tp"), None))
    body = functools.partial(local, mesh.shape["seq"], mesh.shape["tp"])
    return jax.shard_map(body, mesh=mesh, in_specs=in_specs, out_specs=out_specs, check_vma=False)
```

time: 93.6 us -> 65.5 us (0.70)
  Pallas kernels: 85.9 us -> 57.8 us
  local copies, waits for them, and re-layouts: 5.43 us -> 6.84 us
  other arithmetic: 1.32 us -> 0 us
    pallas_call x3 -> x1, Pallas kernels: 85.9 us -> 57.8 us  [local(): pl.pallas_call(functools.partial(kernel, nseq, ntp), out_shape=(big, big,...]
    unnamed x5 -> x10, local copies, waits for them, and re-layouts: 4.53 us -> 6.84 us
    broadcast_in_dim x1 -> x0, other arithmetic: 1.32 us -> none  [local(): skip = jnp.concatenate([skip_gain, skip_gain])[None, :]]
where the time goes in v2:
time: 65.5 us; the launch traced here: 65.3 us
  Pallas kernels  57.8 us (88%)
  local copies, waits for them, and re-layouts  6.84 us (10%)
    pallas_call x1, Pallas kernels, local(): pl.pallas_call(functools.partial(kernel, nseq, ntp), out_shape=(big, big,...  57.8 us
    unnamed x10, local copies, waits for them, and re-layouts  6.84 us

profile of v2, /device:TPU:0, one launch (start us, length us, event | category | flops | bytes accessed | tf_op | source)
XLA Modules:
  0.0 65.3 jit_solution(10373935389888771470)
XLA Ops:
  0.6 57.8 %ssd_layer.1 = (bf16[1024,1536]{1,0:T(8,128)(2,1)}, bf16[1024,1536]{1,0:T(8,128)(2,1)}, bf16[256,128]{1,0:T(8,128)(2,1)}, bf16[256,128]{1,0:T(8,128)(2,1)}) custom-call(bf16[1024,1536]{1,0:T(8,128)(2,1)} %x_hbm.1, bf16[1024,1536]{1,0:T(8,128)(2,1)} %g_hbm.1, bf16[256,128]{1,0:T(8,128)(2,1)} %k_ref.1, bf16[256,128]{1,0:T(8,128)(2,1)} %q_ref.1, ...), custom_call_target="tpu_custom_call" | custom-call | tf_op jit(solution)/shard_map/ssd_layer/pallas_call | solution.py:327
  58.5 0.0 copy-start
  58.5 3.9 %copy.14 = bf16[1024,1536]{1,0:T(8,128)(2,1)} copy(bf16[1024,1536]{1,0:T(8,128)(2,1)} %get-tuple-element.8) | data formatting | bytes 6291456
  62.4 0.0 copy-done
  62.4 0.0 copy-start.2
  62.4 0.0 copy-start.1
  62.4 1.7 %copy.15 = bf16[1024,1536]{1,0:T(8,128)(2,1)} copy(bf16[1024,1536]{1,0:T(8,128)(2,1)S(1)} %copy-done) | data formatting | bytes 6291456
  64.1 0.0 copy-done.2
  64.1 0.6 copy.16
  64.7 0.0 copy-done.1
  64.7 0.6 copy.17
Async XLA Ops:
  58.5 3.9 %copy-start = (bf16[1024,1536]{1,0:T(8,128)(2,1)S(1)}, bf16[1024,1536]{1,0:T(8,128)(2,1)}, u32[]{:S(2)}) copy-start(bf16[1024,1536]{1,0:T(8,128)(2,1)} %get-tuple-element.9) | copy-start | bytes 9437188
  62.4 1.7 %copy-start.2 = (bf16[256,128]{1,0:T(8,128)(2,1)S(1)}, bf16[256,128]{1,0:T(8,128)(2,1)}, u32[]{:S(2)}) copy-start(bf16[256,128]{1,0:T(8,128)(2,1)} %get-tuple-element.10) | copy-start | bytes 196612
  62.4 2.3 %copy-start.1 = (bf16[256,128]{1,0:T(8,128)(2,1)S(1)}, bf16[256,128]{1,0:T(8,128)(2,1)}, u32[]{:S(2)}) copy-start(bf16[256,128]{1,0:T(8,128)(2,1)} %get-tuple-element.11) | copy-start | bytes 196612

commit v3 on v2

--- a/solution.py
+++ b/solution.py
@@ -9,7 +9,6 @@
 CHUNK = 128
 HALF = CHUNK // 2
 LANES = 128
-PIECES = 8
 MESH = pl.DeviceIdType.MESH
 F32 = jnp.float32
 BF16 = jnp.bfloat16
@@ -45,17 +44,23 @@
 def kernel(
     nseq, ntp,
     x_hbm, g_hbm, k_ref, q_ref, ld_ref, skip_ref,
-    mixed_hbm, grad_hbm, wout, rout,
+    mixed_ref, grad_ref, wout, rout,
     x_ref, g_ref, xs_ref, gs_ref, xe_ref, ge_ref, kbuf, qbuf, tsum, csum, factors, ea_ref, eb_ref,
-    srecv, crecv, ssend, csend, fstack, bstack, wpart, rpart, got,
-    load_sem, store_sem, ag_send, ag_recv, st_send, st_recv, ct_send, ct_recv, rs_send, rs_recv,
+    logsum, pairfac, corefac, pair_out, pair_in, sums_out, sums_in, half_out, half_in,
+    fstack, bstack, wpart, rpart, wlocal, rlocal, got,
+    load_sem, ag_send, ag_recv, log_send, log_recv, pair_send, pair_recv, sum_send, sum_recv,
+    half_send, half_recv, rs_send, rs_recv,
 ):
     seq, tp = lax.axis_index("seq"), lax.axis_index("tp")
     rows = k_ref.shape[0]
     tokens, width = x_ref.shape
     chunks = tokens // CHUNK
     per = rows // CHUNK
-    right, left = lax.rem(seq + 1, nseq), lax.rem(seq + nseq - 1, nseq)
+    groups = nseq // 2
+    group = seq // 2
+    core = seq - 2 * group
+    sibling = 2 * group + 1 - core
+    heads = ld_ref.shape[0]
 
     def load(which, c):
         src, dst = ((x_hbm, x_ref), (g_hbm, g_ref))[which]
@@ -74,9 +79,11 @@
         pl.semaphore_signal(
             barrier, inc=1, device_id={"tp": lax.rem(tp + k, ntp)}, device_id_type=MESH
         )
-    for other in (left, right):
-        pl.semaphore_signal(barrier, inc=1, device_id={"seq": other}, device_id_type=MESH)
-    pl.semaphore_wait(barrier, ntp - 1 + 2)
+    for k in range(1, nseq):
+        pl.semaphore_signal(
+            barrier, inc=1, device_id={"seq": lax.rem(seq + k, nseq)}, device_id_type=MESH
+        )
+    pl.semaphore_wait(barrier, ntp - 1 + nseq - 1)
 
     def ag_copy(which, k, place):
         src, dst = ((k_ref, kbuf), (q_ref, qbuf))[which]
@@ -104,10 +111,25 @@
     kinds = (
         1.0 - before,
         before,
-        jnp.ones((chunks, tokens), F32),
         jnp.where(col >= row, before, 0.0),
         jnp.where(col < row + CHUNK, 1.0 - before, 0.0),
     )
+    whole_log = exact_nt(jnp.ones((8, tokens), F32), logs)
+    logsum[seq] = jnp.zeros((8, logsum.shape[2]), F32)
+    logsum[seq, :, 0:heads] = whole_log
+
+    def log_copy(k, place):
+        return pltpu.make_async_remote_copy(
+            src_ref=logsum.at[place],
+            dst_ref=logsum.at[place],
+            send_sem=log_send.at[k],
+            recv_sem=log_recv.at[k],
+            device_id={"seq": lax.rem(seq + k, nseq)},
+            device_id_type=MESH,
+        )
+
+    for k in range(1, nseq):
+        log_copy(k, seq).start()
     for n, kind in enumerate(kinds):
         factors[n * chunks : (n + 1) * chunks, :] = widen(jnp.exp(exact_nt(kind, logs)), width)
 
@@ -137,6 +159,14 @@
 
     lax.fori_loop(0, chunks, scale, 0)
 
+    for k in range(1, nseq):
+        log_copy(k, lax.rem(seq - k + nseq, nseq)).wait_recv()
+    for n in range(groups):
+        both_logs = logsum[2 * n, :, 0:heads] + logsum[2 * n + 1, :, 0:heads]
+        pairfac[8 * n : 8 * n + 8, :] = widen(jnp.exp(both_logs), width)
+    for n in range(2):
+        corefac[8 * n : 8 * n + 8, :] = widen(jnp.exp(logsum[2 * group + n, :, 0:heads]), width)
+
     for k in range(ntp):
         place = lax.rem(tp - k + ntp, ntp)
         if k > 0:
@@ -152,69 +182,106 @@
             tsum[...] += up
             csum[...] += down
 
-    whole = factors[2 * chunks : 2 * chunks + 1, :]
-    step = tsum.shape[0] // PIECES
-
-    def hop(p, out, got_ref, send, recv, nxt):
-        at = rows_at(p, step)
-        return at, pltpu.make_async_remote_copy(
-            src_ref=out.at[at],
-            dst_ref=got_ref.at[at],
-            send_sem=send.at[p],
-            recv_sem=recv.at[p],
-            device_id={"seq": nxt},
+    half = tsum.shape[0] // 2
+    mine, others = rows_at(core, half), rows_at(1 - core, half)
+
+    def to_sibling(n, src, dst, send, recv):
+        return pltpu.make_async_remote_copy(
+            src_ref=src.at[n],
+            dst_ref=dst.at[n],
+            send_sem=send.at[n],
+            recv_sem=recv.at[n],
+            device_id={"seq": sibling},
             device_id_type=MESH,
         )
 
-    def chain(own_sum, got_ref, out, send, recv, first, last, nxt):
-        @pl.when(seq == first)
-        def _():
-            got_ref[...] = jnp.zeros_like(got_ref)
-
-        def piece(p, carry):
-            at, copy = hop(p, out, got_ref, send, recv, nxt)
-
-            @pl.when(seq != first)
-            def _():
-                copy.wait_recv()
-
-            @pl.when(seq != last)
-            def _():
-                out[at, :] = (whole * got_ref[at, :].astype(F32) + own_sum[at, :]).astype(BF16)
-                copy.start()
-
-            return carry
-
-        lax.fori_loop(0, PIECES, piece, 0)
-
-    def states():
-        chain(tsum, srecv, ssend, st_send, st_recv, 0, nseq - 1, right)
-
-    def cotangents():
-        chain(csum, crecv, csend, ct_send, ct_recv, nseq - 1, 0, left)
-
-    early = 2 * seq < nseq
-
-    @pl.when(early)
-    def _():
-        states()
-        cotangents()
-
-    @pl.when(jnp.logical_not(early))
-    def _():
-        cotangents()
-        states()
-
-    tsum[...] = srecv[...].astype(F32)
-    csum[...] = crecv[...].astype(F32)
+    for n, total in enumerate((tsum, csum)):
+        pair_out[n] = total[others, :].astype(BF16)
+        to_sibling(n, pair_out, pair_in, pair_send, pair_recv).start()
+    for n in range(2):
+        to_sibling(n, pair_out, pair_in, pair_send, pair_recv).wait_recv()
+
+    fac0, fac1 = corefac[0:1, :], corefac[8:9, :]
+    is_first = core == 0
+
+    def ordered(n, total):
+        ours, theirs = total[mine, :], pair_in[n].astype(F32)
+        return jnp.where(is_first, ours, theirs), jnp.where(is_first, theirs, ours)
+
+    s0, s1 = ordered(0, tsum)
+    sums_out[0] = (fac1 * s0 + s1).astype(BF16)
+    c0, c1 = ordered(1, csum)
+    sums_out[1] = (fac0 * c1 + c0).astype(BF16)
+
+    def sum_copy(n, k, place):
+        peer = lax.rem(group + k, groups)
+        return pltpu.make_async_remote_copy(
+            src_ref=sums_out.at[n],
+            dst_ref=sums_in.at[place],
+            send_sem=sum_send.at[k],
+            recv_sem=sum_recv.at[place],
+            device_id={"seq": 2 * peer + core},
+            device_id_type=MESH,
+        )
+
+    for k in range(1, groups):
+        later = group + k < groups
+
+        @pl.when(later)
+        def _(k=k):
+            sum_copy(0, k, group).start()
+
+        @pl.when(jnp.logical_not(later))
+        def _(k=k):
+            sum_copy(1, k, group).start()
+
+    def local_grads(c, carry):
+        at = rows_at(c, CHUNK)
+        mixer = lax.dot_general(gs_ref[at, :], xs_ref[at, :], NT, preferred_element_type=F32)
+        mixer = jnp.where(lower, mixer, 0.0).astype(BF16)
+        rlocal[at, :] = jnp.dot(mixer, kbuf[at, :], preferred_element_type=F32)
+        wlocal[at, :] = lax.dot_general(mixer, qbuf[at, :], TN, preferred_element_type=F32)
+        return carry
+
+    lax.fori_loop(0, chunks, local_grads, 0)
+
+    c1_half = jnp.where(is_first, pair_in[1].astype(F32), csum[mine, :])
+    s0_half = jnp.where(is_first, tsum[mine, :], pair_in[0].astype(F32))
+    csum[mine, :] = jnp.zeros((half, width), F32)
+    tsum[mine, :] = jnp.zeros((half, width), F32)
+    for order, total, test in (
+        (range(groups), tsum, lambda n: n < group),
+        (range(groups - 1, -1, -1), csum, lambda n: n > group),
+    ):
+        for n in order:
+
+            @pl.when(test(n))
+            def _(n=n, total=total):
+                sum_copy(0, 1, n).wait_recv()
+                total[mine, :] = (
+                    pairfac[8 * n : 8 * n + 1, :] * total[mine, :] + sums_in[n].astype(F32)
+                )
+
+    s_pair, c_pair = tsum[mine, :], csum[mine, :]
+    s_next = fac0 * s_pair + s0_half
+    c_next = fac1 * c_pair + c1_half
+    half_out[0] = jnp.where(is_first, s_next, s_pair).astype(BF16)
+    half_out[1] = jnp.where(is_first, c_pair, c_next).astype(BF16)
+    for n in range(2):
+        to_sibling(n, half_out, half_in, half_send, half_recv).start()
+    tsum[mine, :] = jnp.where(is_first, s_pair, s_next)
+    csum[mine, :] = jnp.where(is_first, c_next, c_pair)
+    for n, total in enumerate((tsum, csum)):
+        to_sibling(n, half_out, half_in, half_send, half_recv).wait_recv()
+        total[others, :] = half_in[n].astype(F32)
 
     skip = widen(jnp.broadcast_to(skip_ref[...], (8, skip_ref.shape[1])), width)[0:1, :]
 
-    def one(c, flip, left_ref, right_ref, a_ref, b_ref, outer_ref, stack, carry, out, small):
+    def one(c, flip, left_ref, right_ref, a_ref, b_ref, outer_ref, stack, carry, out, small, small_local):
         at = rows_at(c, CHUNK)
         lhs, rhs = left_ref[at, :], right_ref[at, :]
         x = a_ref[at, :]
-        first, second = (factor(4, c), factor(3, c)) if flip else (factor(3, c), factor(4, c))
+        first, second = (factor(3, c), factor(2, c)) if flip else (factor(2, c), factor(3, c))
         mask = upper if flip else lower
         gram = lax.dot_general(lhs, rhs, NT, preferred_element_type=F32)
         gram = jnp.where(mask, gram, 0.0).astype(BF16)
@@ -233,16 +300,8 @@
         outer = widen(outer_ref[at, :], width)
         out[at, :] = (outer * (result[:CHUNK] + skip * x.astype(F32))).astype(BF16)
         carry[...] = second * (low + result[CHUNK:])
-        pair = lax.dot_general(b_ref[at, :], stack[...], NT, preferred_element_type=F32)
-        mixer = jnp.where(mask, pair[:, :CHUNK], 0.0).astype(BF16)
-        small[at, :] = (
-            jnp.dot(mixer, rhs, preferred_element_type=F32) + pair[:, CHUNK:]
-        ).astype(BF16)
-
-    def store(which, c):
-        src, dst = ((xe_ref, mixed_hbm), (ge_ref, grad_hbm))[which]
-        at = rows_at(c, CHUNK)
-        return pltpu.make_async_copy(src.at[at], dst.at[at], store_sem.at[which, c])
+        cross = lax.dot_general(b_ref[at, :], stack[CHUNK:, :], NT, preferred_element_type=F32)
+        small[at, :] = (small_local[at, :] + cross).astype(BF16)
 
     def rs_copy(which, k, j, c, peer):
         src = (rpart, wpart)[which]
@@ -265,10 +324,8 @@
 
     def block(i, carry):
         j = chunks - 1 - i
-        one(i, False, qbuf, kbuf, xs_ref, gs_ref, eb_ref, fstack, tsum, xe_ref, rpart)
-        one(j, True, kbuf, qbuf, gs_ref, xs_ref, ea_ref, bstack, csum, ge_ref, wpart)
-        store(0, i).start()
-        store(1, j).start()
+        one(i, False, qbuf, kbuf, xs_ref, gs_ref, eb_ref, fstack, tsum, mixed_ref, rpart, rlocal)
+        one(j, True, kbuf, qbuf, gs_ref, xs_ref, ea_ref, bstack, csum, grad_ref, wpart, wlocal)
         send_part(0, i)
         send_part(1, j)
         return carry
@@ -290,24 +347,13 @@
                 peer = lax.rem(tp + k, ntp)
                 rs_copy(which, k, j, peer * per + j, peer).wait_send()
 
-    def finish(c, carry):
-        store(0, c).wait()
-        store(1, c).wait()
-        return carry
-
-    lax.fori_loop(0, chunks, finish, 0)
-
-    def drain(out, got_ref, send, recv, nxt, last):
-        @pl.when(seq != last)
-        def _():
-            def one_piece(p, carry):
-                hop(p, out, got_ref, send, recv, nxt)[1].wait_send()
-                return carry
-
-            lax.fori_loop(0, PIECES, one_piece, 0)
-
-    drain(ssend, srecv, st_send, st_recv, right, nseq - 1)
-    drain(csend, crecv, ct_send, ct_recv, left, 0)
+    for k in range(1, nseq):
+        log_copy(k, seq).wait_send()
+    for n in range(2):
+        to_sibling(n, pair_out, pair_in, pair_send, pair_recv).wait_send()
+        to_sibling(n, half_out, half_in, half_send, half_recv).wait_send()
+    for k in range(1, groups):
+        sum_copy(0, k, group).wait_send()
 
 
 def local(nseq, ntp, head_inputs, write_keys, read_queries, log_decay, skip_gain, out_grad):
@@ -318,23 +364,29 @@
     vmem = pl.BlockSpec(memory_space=pltpu.VMEM)
     hbm = pl.BlockSpec(memory_space=pl.ANY)
     dma = pltpu.SemaphoreType.DMA
-    big = jax.ShapeDtypeStruct((tokens, width), BF16)
-    part = jax.ShapeDtypeStruct((rows, size), BF16)
+    big = pltpu.VMEM((tokens, width), BF16)
+    part = pltpu.VMEM((rows, size), BF16)
     wide, tall = pltpu.VMEM((tokens, width), BF16), pltpu.VMEM((tokens, size), BF16)
-    edge, total = pltpu.VMEM((size, width), BF16), pltpu.VMEM((size, width), F32)
+    total = pltpu.VMEM((size, width), F32)
+    halves = pltpu.VMEM((2, size // 2, width), BF16)
+    small = pltpu.VMEM((tokens, size), F32)
+    groups = nseq // 2
+    lanes = -(-heads // LANES) * LANES
     by_head = pltpu.VMEM((tokens, heads), F32)
     stack = pltpu.VMEM((CHUNK + size, width), BF16)
     return pl.pallas_call(
         functools.partial(kernel, nseq, ntp),
         out_shape=(big, big, part, part),
         in_specs=[hbm, hbm, vmem, vmem, vmem, vmem],
-        out_specs=[hbm, hbm, vmem, vmem],
+        out_specs=[vmem] * 4,
         scratch_shapes=[wide] * 6
-        + [tall, tall, total, total, pltpu.VMEM((5 * chunks, width), F32), by_head, by_head]
-        + [edge] * 4
-        + [stack, stack, tall, tall, pltpu.VMEM((2, ntp - 1, rows, size), BF16)]
-        + [dma((2, chunks)), dma((2, chunks)), dma((2, ntp)), dma((2, ntp))]
-        + [dma((PIECES,))] * 4
+        + [tall, tall, total, total, pltpu.VMEM((4 * chunks, width), F32), by_head, by_head]
+        + [pltpu.VMEM((nseq, 8, lanes), F32)]
+        + [pltpu.VMEM((8 * groups, width), F32), pltpu.VMEM((16, width), F32)]
+        + [halves, halves, halves, pltpu.VMEM((groups, size // 2, width), BF16), halves, halves]
+        + [stack, stack, tall, tall, small, small, pltpu.VMEM((2, ntp - 1, rows, size), BF16)]
+        + [dma((2, chunks)), dma((2, ntp)), dma((2, ntp)), dma((nseq,)), dma((nseq,))]
+        + [dma((2,)), dma((2,)), dma((groups,)), dma((groups,)), dma((2,)), dma((2,))]
         + [dma((2, ntp - 1, rows // CHUNK))] * 2,
         compiler_params=pltpu.CompilerParams(
             collective_id=0, has_side_effects=True, vmem_limit_bytes=LIMIT

time: 65.5 us -> 53.7 us (0.82)
  Pallas kernels: 57.8 us -> 48.3 us
  local copies, waits for them, and re-layouts: 6.84 us -> 4.59 us
    pallas_call x1, Pallas kernels: 57.8 us -> 48.3 us  [local(): pl.pallas_call(functools.partial(kernel, nseq, ntp), out_shape=(big, big,...]
    unnamed x10 -> x4, local copies, waits for them, and re-layouts: 6.84 us -> 4.59 us
where the time goes in v3:
time: 53.7 us; the launch traced here: 53.5 us
  Pallas kernels  48.3 us (90%)
  local copies, waits for them, and re-layouts  4.59 us (9%)
  between operations  0.64 us (1%)
    pallas_call x1, Pallas kernels, local(): pl.pallas_call(functools.partial(kernel, nseq, ntp), out_shape=(big, big,...  48.3 us
    unnamed x4, local copies, waits for them, and re-layouts  4.59 us

profile of v3, /device:TPU:0, one launch (start us, length us, event | category | flops | bytes accessed | tf_op | source)
XLA Modules:
  0.0 53.5 jit_solution(14027700252437170392)
XLA Ops:
  0.6 48.3 %ssd_layer.1 = (bf16[1024,1536]{1,0:T(8,128)(2,1)S(1)}, bf16[1024,1536]{1,0:T(8,128)(2,1)S(1)}, bf16[256,128]{1,0:T(8,128)(2,1)S(1)}, bf16[256,128]{1,0:T(8,128)(2,1)S(1)}) custom-call(bf16[1024,1536]{1,0:T(8,128)(2,1)} %x_hbm.1, bf16[1024,1536]{1,0:T(8,128)(2,1)} %g_hbm.1, bf16[256,128]{1,0:T(8,128)(2,1)} %k_ref.1, bf16[256,128]{1,0:T(8,128)(2,1)} %q_ref.1, ...), custom_call_target="tpu_custom_call" | custom-call | tf_op jit(solution)/shard_map/ssd_layer/pallas_call | solution.py:377
  48.9 1.7 %copy.14 = bf16[1024,1536]{1,0:T(8,128)(2,1)} copy(bf16[1024,1536]{1,0:T(8,128)(2,1)S(1)} %get-tuple-element.4) | data formatting | bytes 6291456
  50.6 0.6 %copy.16 = bf16[256,128]{1,0:T(8,128)(2,1)} copy(bf16[256,128]{1,0:T(8,128)(2,1)S(1)} %get-tuple-element.6) | data formatting | bytes 131072
  51.2 0.6 %copy.17 = bf16[256,128]{1,0:T(8,128)(2,1)} copy(bf16[256,128]{1,0:T(8,128)(2,1)S(1)} %get-tuple-element.7) | data formatting | bytes 131072
  51.8 1.7 %copy.15 = bf16[1024,1536]{1,0:T(8,128)(2,1)} copy(bf16[1024,1536]{1,0:T(8,128)(2,1)S(1)} %get-tuple-element.5) | data formatting | bytes 6291456

commit v4 on v3

--- a/solution.py
+++ b/solution.py
@@ -47,7 +47,7 @@
     mixed_ref, grad_ref, wout, rout,
     x_ref, g_ref, xs_ref, gs_ref, xe_ref, ge_ref, kbuf, qbuf, tsum, csum, factors, ea_ref, eb_ref,
     logsum, pairfac, corefac, pair_out, pair_in, sums_out, sums_in, half_out, half_in,
-    fstack, bstack, wpart, rpart, wlocal, rlocal, got,
+    fstack, bstack, wpart, rpart, wlocal, rlocal, sadd, cadd, got,
     load_sem, ag_send, ag_recv, log_send, log_recv, pair_send, pair_recv, sum_send, sum_recv,
     half_send, half_recv, rs_send, rs_recv,
 ):
@@ -96,8 +96,8 @@
             device_id_type=MESH,
         )
 
-    for k in range(ntp - 1, 0, -1):
-        for which in range(2):
+    for which in range(2):
+        for k in range(ntp - 1, 0, -1):
             ag_copy(which, k, tp).start()
 
     own = rows_at(tp, rows)
@@ -141,23 +141,20 @@
     lower, upper = trow >= tcol, trow <= tcol
     about_middle = jnp.where(lower, 1.0, 0.0) - jnp.where(tcol < HALF, 1.0, 0.0)
 
-    def scale(c, carry):
+    def scale(which, c, carry):
+        src, dst, end = ((x_ref, xs_ref, xe_ref), (g_ref, gs_ref, ge_ref))[which]
         at = rows_at(c, CHUNK)
         d = exact_nt(about_middle, ld_ref[:, at])
-        a, b = jnp.exp(-d), jnp.exp(d)
-        ea_ref[at, :] = a
-        eb_ref[at, :] = b
-        load(0, c).wait()
-        x = x_ref[at, :].astype(F32) * widen(a, width)
-        xs_ref[at, :] = x.astype(BF16)
-        xe_ref[at, :] = (x * factor(0, c)).astype(BF16)
-        load(1, c).wait()
-        g = g_ref[at, :].astype(F32) * widen(b, width)
-        gs_ref[at, :] = g.astype(BF16)
-        ge_ref[at, :] = (g * factor(1, c)).astype(BF16)
-        return carry
-
-    lax.fori_loop(0, chunks, scale, 0)
+        spread = jnp.exp(d if which else -d)
+        (eb_ref if which else ea_ref)[at, :] = spread
+        load(which, c).wait()
+        value = src[at, :].astype(F32) * widen(spread, width)
+        dst[at, :] = value.astype(BF16)
+        end[at, :] = (value * factor(which, c)).astype(BF16)
+        return carry
+
+    scale_inputs, scale_grads = functools.partial(scale, 0), functools.partial(scale, 1)
+    lax.fori_loop(0, chunks, scale_inputs, 0)
 
     for k in range(1, nseq):
         log_copy(k, lax.rem(seq - k + nseq, nseq)).wait_recv()
@@ -167,23 +164,10 @@
     for n in range(2):
         corefac[8 * n : 8 * n + 8, :] = widen(jnp.exp(logsum[2 * group + n, :, 0:heads]), width)
 
-    for k in range(ntp):
-        place = lax.rem(tp - k + ntp, ntp)
-        if k > 0:
-            for which in range(2):
-                ag_copy(which, k, place).wait_recv()
-        at = rows_at(place, rows)
-        up = lax.dot_general(kbuf[at, :], xe_ref[at, :], TN, preferred_element_type=F32)
-        down = lax.dot_general(qbuf[at, :], ge_ref[at, :], TN, preferred_element_type=F32)
-        if k == 0:
-            tsum[...] = up
-            csum[...] = down
-        else:
-            tsum[...] += up
-            csum[...] += down
-
     half = tsum.shape[0] // 2
     mine, others = rows_at(core, half), rows_at(1 - core, half)
+    fac0, fac1 = corefac[0:1, :], corefac[8:9, :]
+    is_first = core == 0
 
     def to_sibling(n, src, dst, send, recv):
         return pltpu.make_async_remote_copy(
@@ -195,23 +179,11 @@
             device_id_type=MESH,
         )
 
-    for n, total in enumerate((tsum, csum)):
-        pair_out[n] = total[others, :].astype(BF16)
-        to_sibling(n, pair_out, pair_in, pair_send, pair_recv).start()
-    for n in range(2):
-        to_sibling(n, pair_out, pair_in, pair_send, pair_recv).wait_recv()
-
-    fac0, fac1 = corefac[0:1, :], corefac[8:9, :]
-    is_first = core == 0
-
-    def ordered(n, total):
-        ours, theirs = total[mine, :], pair_in[n].astype(F32)
-        return jnp.where(is_first, ours, theirs), jnp.where(is_first, theirs, ours)
-
-    s0, s1 = ordered(0, tsum)
-    sums_out[0] = (fac1 * s0 + s1).astype(BF16)
-    c0, c1 = ordered(1, csum)
-    sums_out[1] = (fac0 * c1 + c0).astype(BF16)
+    def pair_copy(n):
+        return to_sibling(n, pair_out, pair_in, pair_send, pair_recv)
+
+    def half_copy(n):
+        return to_sibling(n, half_out, half_in, half_send, half_recv)
 
     def sum_copy(n, k, place):
         peer = lax.rem(group + k, groups)
@@ -224,16 +196,63 @@
             device_id_type=MESH,
         )
 
-    for k in range(1, groups):
-        later = group + k < groups
-
-        @pl.when(later)
-        def _(k=k):
-            sum_copy(0, k, group).start()
-
-        @pl.when(jnp.logical_not(later))
-        def _(k=k):
-            sum_copy(1, k, group).start()
+    def end_sum(which):
+        buf, scaled, total = ((kbuf, xe_ref, tsum), (qbuf, ge_ref, csum))[which]
+        for k in range(ntp):
+            place = lax.rem(tp - k + ntp, ntp)
+            if k > 0:
+                ag_copy(which, k, place).wait_recv()
+            at = rows_at(place, rows)
+            term = lax.dot_general(buf[at, :], scaled[at, :], TN, preferred_element_type=F32)
+            if k == 0:
+                total[...] = term
+            else:
+                total[...] += term
+        pair_out[which] = total[others, :].astype(BF16)
+        pair_copy(which).start()
+
+    def send_sums(which):
+        total = (tsum, csum)[which]
+        pair_copy(which).wait_recv()
+        ours, theirs = total[mine, :], pair_in[which].astype(F32)
+        zeroth, first = jnp.where(is_first, ours, theirs), jnp.where(is_first, theirs, ours)
+        joined = fac0 * first + zeroth if which else fac1 * zeroth + first
+        sums_out[which] = joined.astype(BF16)
+        for k in range(1, groups):
+            later = group + k < groups
+
+            @pl.when(jnp.logical_not(later) if which else later)
+            def _(k=k):
+                sum_copy(which, k, group).start()
+
+    def enter(which):
+        total = (tsum, csum)[which]
+        received = pair_in[which].astype(F32)
+        own_half = total[mine, :]
+        total[mine, :] = jnp.zeros((half, width), F32)
+        for n in range(groups - 1, -1, -1) if which else range(groups):
+
+            @pl.when(n > group if which else n < group)
+            def _(n=n):
+                sum_copy(0, 1, n).wait_recv()
+                total[mine, :] = (
+                    pairfac[8 * n : 8 * n + 1, :] * total[mine, :] + sums_in[n].astype(F32)
+                )
+
+        into = total[mine, :]
+        if which:
+            beyond = fac1 * into + jnp.where(is_first, received, own_half)
+            half_out[1] = jnp.where(is_first, into, beyond).astype(BF16)
+            total[mine, :] = jnp.where(is_first, beyond, into)
+        else:
+            beyond = fac0 * into + jnp.where(is_first, own_half, received)
+            half_out[0] = jnp.where(is_first, beyond, into).astype(BF16)
+            total[mine, :] = jnp.where(is_first, into, beyond)
+        half_copy(which).start()
+
+    def complete(which):
+        half_copy(which).wait_recv()
+        (tsum, csum)[which][others, :] = half_in[which].astype(F32)
 
     def local_grads(c, carry):
         at = rows_at(c, CHUNK)
@@ -243,41 +262,27 @@
         wlocal[at, :] = lax.dot_general(mixer, qbuf[at, :], TN, preferred_element_type=F32)
         return carry
 
-    lax.fori_loop(0, chunks, local_grads, 0)
-
-    c1_half = jnp.where(is_first, pair_in[1].astype(F32), csum[mine, :])
-    s0_half = jnp.where(is_first, tsum[mine, :], pair_in[0].astype(F32))
-    csum[mine, :] = jnp.zeros((half, width), F32)
-    tsum[mine, :] = jnp.zeros((half, width), F32)
-    for order, total, test in (
-        (range(groups), tsum, lambda n: n < group),
-        (range(groups - 1, -1, -1), csum, lambda n: n > group),
-    ):
-        for n in order:
-
-            @pl.when(test(n))
-            def _(n=n, total=total):
-                sum_copy(0, 1, n).wait_recv()
-                total[mine, :] = (
-                    pairfac[8 * n : 8 * n + 1, :] * total[mine, :] + sums_in[n].astype(F32)
-                )
-
-    s_pair, c_pair = tsum[mine, :], csum[mine, :]
-    s_next = fac0 * s_pair + s0_half
-    c_next = fac1 * c_pair + c1_half
-    half_out[0] = jnp.where(is_first, s_next, s_pair).astype(BF16)
-    half_out[1] = jnp.where(is_first, c_pair, c_next).astype(BF16)
-    for n in range(2):
-        to_sibling(n, half_out, half_in, half_send, half_recv).start()
-    tsum[mine, :] = jnp.where(is_first, s_pair, s_next)
-    csum[mine, :] = jnp.where(is_first, c_next, c_pair)
-    for n, total in enumerate((tsum, csum)):
-        to_sibling(n, half_out, half_in, half_send, half_recv).wait_recv()
-        total[others, :] = half_in[n].astype(F32)
+    def updates(c, carry):
+        at = rows_at(c, CHUNK)
+        sadd[c] = lax.dot_general(kbuf[at, :], xs_ref[at, :], TN, preferred_element_type=F32)
+        cadd[c] = lax.dot_general(qbuf[at, :], gs_ref[at, :], TN, preferred_element_type=F32)
+        return carry
+
+    middle = chunks // 2
+    end_sum(0)
+    lax.fori_loop(0, middle, scale_grads, 0)
+    send_sums(0)
+    lax.fori_loop(middle, chunks, scale_grads, 0)
+    end_sum(1)
+    lax.fori_loop(0, middle, local_grads, 0)
+    send_sums(1)
+    lax.fori_loop(middle, chunks, local_grads, 0)
+    lax.fori_loop(0, chunks, updates, 0)
+    enter(0)
 
     skip = widen(jnp.broadcast_to(skip_ref[...], (8, skip_ref.shape[1])), width)[0:1, :]
 
-    def one(c, flip, left_ref, right_ref, a_ref, b_ref, outer_ref, stack, carry, out, small, small_local):
+    def one(c, flip, left_ref, right_ref, a_ref, b_ref, outer_ref, stack, carry, add, out, small, small_local):
         at = rows_at(c, CHUNK)
         lhs, rhs = left_ref[at, :], right_ref[at, :]
         x = a_ref[at, :]
@@ -288,18 +293,12 @@
         low = first * carry[...]
         stack[0:CHUNK, :] = x
         stack[CHUNK:, :] = low.astype(BF16)
-        turned = rhs.astype(F32).T.astype(BF16)
-        both = jnp.concatenate(
-            [
-                jnp.concatenate([gram, lhs], axis=1),
-                jnp.concatenate([turned, jnp.zeros((turned.shape[0], lhs.shape[1]), BF16)], axis=1),
-            ],
-            axis=0,
-        )
-        result = jnp.dot(both, stack[...], preferred_element_type=F32)
+        total = jnp.dot(
+            jnp.concatenate([gram, lhs], axis=1), stack[...], preferred_element_type=F32
+        )
         outer = widen(outer_ref[at, :], width)
-        out[at, :] = (outer * (result[:CHUNK] + skip * x.astype(F32))).astype(BF16)
-        carry[...] = second * (low + result[CHUNK:])
+        out[at, :] = (outer * (total + skip * x.astype(F32))).astype(BF16)
+        carry[...] = second * (low + add[c])
         cross = lax.dot_general(b_ref[at, :], stack[CHUNK:, :], NT, preferred_element_type=F32)
         small[at, :] = (small_local[at, :] + cross).astype(BF16)
 
@@ -322,15 +321,24 @@
         def _():
             rs_copy(which, k, c - peer * per, c, peer).start()
 
-    def block(i, carry):
-        j = chunks - 1 - i
-        one(i, False, qbuf, kbuf, xs_ref, gs_ref, eb_ref, fstack, tsum, mixed_ref, rpart, rlocal)
-        one(j, True, kbuf, qbuf, gs_ref, xs_ref, ea_ref, bstack, csum, grad_ref, wpart, wlocal)
-        send_part(0, i)
-        send_part(1, j)
-        return carry
-
-    lax.fori_loop(0, chunks, block, 0)
+    def forward(c, carry):
+        one(c, False, qbuf, kbuf, xs_ref, gs_ref, eb_ref, fstack, tsum, sadd, mixed_ref, rpart, rlocal)
+        send_part(0, c)
+        return carry
+
+    def backward(i, carry):
+        c = chunks - 1 - i
+        one(c, True, kbuf, qbuf, gs_ref, xs_ref, ea_ref, bstack, csum, cadd, grad_ref, wpart, wlocal)
+        send_part(1, c)
+        return carry
+
+    late = chunks - chunks // 4
+    complete(0)
+    lax.fori_loop(0, late, forward, 0)
+    enter(1)
+    lax.fori_loop(late, chunks, forward, 0)
+    complete(1)
+    lax.fori_loop(0, chunks, backward, 0)
 
     for which, (src, out) in enumerate(((rpart, rout), (wpart, wout))):
         total = src[own, :].astype(F32)
@@ -350,10 +358,19 @@
     for k in range(1, nseq):
         log_copy(k, seq).wait_send()
     for n in range(2):
-        to_sibling(n, pair_out, pair_in, pair_send, pair_recv).wait_send()
-        to_sibling(n, half_out, half_in, half_send, half_recv).wait_send()
+        pair_copy(n).wait_send()
+        half_copy(n).wait_send()
     for k in range(1, groups):
         sum_copy(0, k, group).wait_send()
+
+
+def store_kernel(*refs):
+    sems = refs[-1]
+    copies = [pltpu.make_async_copy(refs[n], refs[4 + n], sems.at[n]) for n in range(4)]
+    for copy in copies:
+        copy.start()
+    for copy in copies:
+        copy.wait()
 
 
 def local(nseq, ntp, head_inputs, write_keys, read_queries, log_decay, skip_gain, out_grad):
@@ -370,11 +387,12 @@
     total = pltpu.VMEM((size, width), F32)
     halves = pltpu.VMEM((2, size // 2, width), BF16)
     small = pltpu.VMEM((tokens, size), F32)
+    adds = pltpu.VMEM((chunks, size, width), F32)
     groups = nseq // 2
     lanes = -(-heads // LANES) * LANES
     by_head = pltpu.VMEM((tokens, heads), F32)
     stack = pltpu.VMEM((CHUNK + size, width), BF16)
-    return pl.pallas_call(
+    results = pl.pallas_call(
         functools.partial(kernel, nseq, ntp),
         out_shape=(big, big, part, part),
         in_specs=[hbm, hbm, vmem, vmem, vmem, vmem],
@@ -384,7 +402,7 @@
         + [pltpu.VMEM((nseq, 8, lanes), F32)]
         + [pltpu.VMEM((8 * groups, width), F32), pltpu.VMEM((16, width), F32)]
         + [halves, halves, halves, pltpu.VMEM((groups, size // 2, width), BF16), halves, halves]
-        + [stack, stack, tall, tall, small, small, pltpu.VMEM((2, ntp - 1, rows, size), BF16)]
+        + [stack, stack, tall, tall, small, small, adds, adds, pltpu.VMEM((2, ntp - 1, rows, size), BF16)]
         + [dma((2, chunks)), dma((2, ntp)), dma((2, ntp)), dma((nseq,)), dma((nseq,))]
         + [dma((2,)), dma((2,)), dma((groups,)), dma((groups,)), dma((2,)), dma((2,))]
         + [dma((2, ntp - 1, rows // CHUNK))] * 2,
@@ -393,6 +411,14 @@
         ),
         name="ssd_layer",
     )(head_inputs, out_grad, write_keys, read_queries, log_decay, skip_gain[None, :])
+    return pl.pallas_call(
+        store_kernel,
+        out_shape=tuple(jax.ShapeDtypeStruct(r.shape, r.dtype) for r in results),
+        in_specs=[vmem] * 4,
+        out_specs=[hbm] * 4,
+        scratch_shapes=[dma((4,))],
+        name="store_results",
+    )(*results)
 
 
 def solution(mesh):

time: 53.7 us -> 59.3 us (1.10)
  Pallas kernels: 48.3 us -> 53.9 us
    pallas_call x0 -> x1, Pallas kernels: none -> 5.6 us  [local(): pl.pallas_call(store_kernel, out_shape=tuple((jax.ShapeDtypeStruct(r.shap...]
    unnamed x4 -> x8, local copies, waits for them, and re-layouts: 4.59 us -> 4.57 us
where the time goes in v4:
time: 59.3 us; the launch traced here: 59.1 us
  Pallas kernels  53.9 us (91%)
  local copies, waits for them, and re-layouts  4.57 us (8%)
  between operations  0.65 us (1%)
    pallas_call x1, Pallas kernels, local(): pl.pallas_call(functools.partial(kernel, nseq, ntp), out_shape=(big, big,...  48.3 us
    pallas_call x1, Pallas kernels, local(): pl.pallas_call(store_kernel, out_shape=tuple((jax.ShapeDtypeStruct(r.shap...  5.6 us
    unnamed x8, local copies, waits for them, and re-layouts  4.57 us

profile of v4, /device:TPU:0, one launch (start us, length us, event | category | flops | bytes accessed | tf_op | source)
XLA Modules:
  0.0 59.1 jit_solution(9660583103451434702)
XLA Ops:
  0.6 48.3 %ssd_layer.1 = (bf16[1024,1536]{1,0:T(8,128)(2,1)S(1)}, bf16[1024,1536]{1,0:T(8,128)(2,1)S(1)}, bf16[256,128]{1,0:T(8,128)(2,1)S(1)}, bf16[256,128]{1,0:T(8,128)(2,1)S(1)}) custom-call(bf16[1024,1536]{1,0:T(8,128)(2,1)} %x_hbm.1, bf16[1024,1536]{1,0:T(8,128)(2,1)} %g_hbm.1, bf16[256,128]{1,0:T(8,128)(2,1)} %k_ref.1, bf16[256,128]{1,0:T(8,128)(2,1)} %q_ref.1, ...), custom_call_target="tpu_custom_call" | custom-call | tf_op jit(solution)/shard_map/ssd_layer/pallas_call | solution.py:395
  48.9 0.0 copy-start
  48.9 1.6 %copy-done = bf16[1024,1536]{1,0:T(8,128)(2,1)} copy-done((bf16[1024,1536]{1,0:T(8,128)(2,1)}, bf16[1024,1536]{1,0:T(8,128)(2,1)S(1)}, u32[]{:S(2)}) %copy-start) | copy-done | bytes 3145752
  50.6 0.0 copy-start.1
  50.6 1.7 %copy-done.1 = bf16[1024,1536]{1,0:T(8,128)(2,1)} copy-done((bf16[1024,1536]{1,0:T(8,128)(2,1)}, bf16[1024,1536]{1,0:T(8,128)(2,1)S(1)}, u32[]{:S(2)}) %copy-start.1) | copy-done | bytes 3145752
  52.2 0.0 copy-start.2
  52.2 0.6 %copy-done.2 = bf16[256,128]{1,0:T(8,128)(2,1)} copy-done((bf16[256,128]{1,0:T(8,128)(2,1)}, bf16[256,128]{1,0:T(8,128)(2,1)S(1)}, u32[]{:S(2)}) %copy-start.2) | copy-done | bytes 65560
  52.9 0.0 copy-start.3
  52.9 0.6 %copy-done.3 = bf16[256,128]{1,0:T(8,128)(2,1)} copy-done((bf16[256,128]{1,0:T(8,128)(2,1)}, bf16[256,128]{1,0:T(8,128)(2,1)S(1)}, u32[]{:S(2)}) %copy-start.3) | copy-done | bytes 65560
  53.5 5.6 %store_results.1 = (bf16[1024,1536]{1,0:T(8,128)(2,1)}, bf16[1024,1536]{1,0:T(8,128)(2,1)}, bf16[256,128]{1,0:T(8,128)(2,1)}, bf16[256,128]{1,0:T(8,128)(2,1)}) custom-call(bf16[1024,1536]{1,0:T(8,128)(2,1)} %copy-done, bf16[1024,1536]{1,0:T(8,128)(2,1)} %copy-done.1, bf16[256,128]{1,0:T(8,128)(2,1)} %copy-done.2, bf16[256,128]{1,0:T(8,128)(2,1)} %copy-done.3), custom_call_target="tpu_custom_call" | custom-call | tf_op jit(solution)/shard_map/store_results/pallas_call | solution.py:414
Async XLA Ops:
  48.9 1.6 %copy-start = (bf16[1024,1536]{1,0:T(8,128)(2,1)}, bf16[1024,1536]{1,0:T(8,128)(2,1)S(1)}, u32[]{:S(2)}) copy-start(bf16[1024,1536]{1,0:T(8,128)(2,1)S(1)} %get-tuple-element.8.refs_0_) | copy-start | bytes 9437188
  50.6 1.7 %copy-start.1 = (bf16[1024,1536]{1,0:T(8,128)(2,1)}, bf16[1024,1536]{1,0:T(8,128)(2,1)S(1)}, u32[]{:S(2)}) copy-start(bf16[1024,1536]{1,0:T(8,128)(2,1)S(1)} %get-tuple-element.9.refs_1_) | copy-start | bytes 9437188
  52.2 0.6 %copy-start.2 = (bf16[256,128]{1,0:T(8,128)(2,1)}, bf16[256,128]{1,0:T(8,128)(2,1)S(1)}, u32[]{:S(2)}) copy-start(bf16[256,128]{1,0:T(8,128)(2,1)S(1)} %get-tuple-element.10.refs_2_) | copy-start | bytes 196612
  52.9 0.6 %copy-start.3 = (bf16[256,128]{1,0:T(8,128)(2,1)}, bf16[256,128]{1,0:T(8,128)(2,1)S(1)}, u32[]{:S(2)}) copy-start(bf16[256,128]{1,0:T(8,128)(2,1)S(1)} %get-tuple-element.11.refs_3_) | copy-start | bytes 196612

commit v5 on v4

--- a/solution.py
+++ b/solution.py
@@ -45,15 +45,15 @@
     nseq, ntp,
     x_hbm, g_hbm, k_ref, q_ref, ld_ref, skip_ref,
     mixed_ref, grad_ref, wout, rout,
-    x_ref, g_ref, xs_ref, gs_ref, xe_ref, ge_ref, kbuf, qbuf, tsum, csum, factors, ea_ref, eb_ref,
+    xs_ref, gs_ref, xe_ref, ge_ref, kbuf, qbuf, tsum, csum, factors, ea_ref, eb_ref,
     logsum, pairfac, corefac, pair_out, pair_in, sums_out, sums_in, half_out, half_in,
-    fstack, bstack, wpart, rpart, wlocal, rlocal, sadd, cadd, got,
+    fstack0, bstack0, fstack1, bstack1, wpart, rpart, wlocal, rlocal, sadd, cadd, got,
     load_sem, ag_send, ag_recv, log_send, log_recv, pair_send, pair_recv, sum_send, sum_recv,
     half_send, half_recv, rs_send, rs_recv,
 ):
     seq, tp = lax.axis_index("seq"), lax.axis_index("tp")
     rows = k_ref.shape[0]
-    tokens, width = x_ref.shape
+    tokens, width = xs_ref.shape
     chunks = tokens // CHUNK
     per = rows // CHUNK
     groups = nseq // 2
@@ -63,7 +63,7 @@
     heads = ld_ref.shape[0]
 
     def load(which, c):
-        src, dst = ((x_hbm, x_ref), (g_hbm, g_ref))[which]
+        src, dst = ((x_hbm, xe_ref), (g_hbm, ge_ref))[which]
         at = rows_at(c, CHUNK)
         return pltpu.make_async_copy(src.at[at], dst.at[at], load_sem.at[which, c])
 
@@ -142,13 +142,13 @@
     about_middle = jnp.where(lower, 1.0, 0.0) - jnp.where(tcol < HALF, 1.0, 0.0)
 
     def scale(which, c, carry):
-        src, dst, end = ((x_ref, xs_ref, xe_ref), (g_ref, gs_ref, ge_ref))[which]
+        dst, end = ((xs_ref, xe_ref), (gs_ref, ge_ref))[which]
         at = rows_at(c, CHUNK)
         d = exact_nt(about_middle, ld_ref[:, at])
-        spread = jnp.exp(d if which else -d)
+        spread = widen(jnp.exp(d if which else -d), width)
         (eb_ref if which else ea_ref)[at, :] = spread
         load(which, c).wait()
-        value = src[at, :].astype(F32) * widen(spread, width)
+        value = end[at, :].astype(F32) * spread
         dst[at, :] = value.astype(BF16)
         end[at, :] = (value * factor(which, c)).astype(BF16)
         return carry
@@ -296,8 +296,7 @@
         total = jnp.dot(
             jnp.concatenate([gram, lhs], axis=1), stack[...], preferred_element_type=F32
         )
-        outer = widen(outer_ref[at, :], width)
-        out[at, :] = (outer * (total + skip * x.astype(F32))).astype(BF16)
+        out[at, :] = (outer_ref[at, :] * (total + skip * x.astype(F32))).astype(BF16)
         carry[...] = second * (low + add[c])
         cross = lax.dot_general(b_ref[at, :], stack[CHUNK:, :], NT, preferred_element_type=F32)
         small[at, :] = (small_local[at, :] + cross).astype(BF16)
@@ -321,24 +320,28 @@
         def _():
             rs_copy(which, k, c - peer * per, c, peer).start()
 
-    def forward(c, carry):
-        one(c, False, qbuf, kbuf, xs_ref, gs_ref, eb_ref, fstack, tsum, sadd, mixed_ref, rpart, rlocal)
-        send_part(0, c)
+    def forward(c, stack):
+        one(c, False, qbuf, kbuf, xs_ref, gs_ref, eb_ref, stack, tsum, sadd, mixed_ref, rpart, rlocal)
+
+    def backward(c, stack):
+        one(c, True, kbuf, qbuf, gs_ref, xs_ref, ea_ref, stack, csum, cadd, grad_ref, wpart, wlocal)
+
+    def two_blocks(m, carry):
+        i, j = 2 * m, chunks - 1 - 2 * m
+        forward(i, fstack0)
+        backward(j, bstack0)
+        forward(i + 1, fstack1)
+        backward(j - 1, bstack1)
+        send_part(0, i)
+        send_part(1, j)
+        send_part(0, i + 1)
+        send_part(1, j - 1)
         return carry
 
-    def backward(i, carry):
-        c = chunks - 1 - i
-        one(c, True, kbuf, qbuf, gs_ref, xs_ref, ea_ref, bstack, csum, cadd, grad_ref, wpart, wlocal)
-        send_part(1, c)
-        return carry
-
-    late = chunks - chunks // 4
+    enter(1)
     complete(0)
-    lax.fori_loop(0, late, forward, 0)
-    enter(1)
-    lax.fori_loop(late, chunks, forward, 0)
     complete(1)
-    lax.fori_loop(0, chunks, backward, 0)
+    lax.fori_loop(0, chunks // 2, two_blocks, 0)
 
     for which, (src, out) in enumerate(((rpart, rout), (wpart, wout))):
         total = src[own, :].astype(F32)
@@ -362,15 +365,6 @@
         half_copy(n).wait_send()
     for k in range(1, groups):
         sum_copy(0, k, group).wait_send()
-
-
-def store_kernel(*refs):
-    sems = refs[-1]
-    copies = [pltpu.make_async_copy(refs[n], refs[4 + n], sems.at[n]) for n in range(4)]
-    for copy in copies:
-        copy.start()
-    for copy in copies:
-        copy.wait()
 
 
 def local(nseq, ntp, head_inputs, write_keys, read_queries, log_decay, skip_gain, out_grad):
@@ -390,19 +384,20 @@
     adds = pltpu.VMEM((chunks, size, width), F32)
     groups = nseq // 2
     lanes = -(-heads // LANES) * LANES
-    by_head = pltpu.VMEM((tokens, heads), F32)
+    outer = pltpu.VMEM((tokens, width), F32)
     stack = pltpu.VMEM((CHUNK + size, width), BF16)
-    results = pl.pallas_call(
+    return pl.pallas_call(
         functools.partial(kernel, nseq, ntp),
         out_shape=(big, big, part, part),
         in_specs=[hbm, hbm, vmem, vmem, vmem, vmem],
         out_specs=[vmem] * 4,
-        scratch_shapes=[wide] * 6
-        + [tall, tall, total, total, pltpu.VMEM((4 * chunks, width), F32), by_head, by_head]
+        scratch_shapes=[wide] * 4
+        + [tall, tall, total, total, pltpu.VMEM((4 * chunks, width), F32), outer, outer]
         + [pltpu.VMEM((nseq, 8, lanes), F32)]
         + [pltpu.VMEM((8 * groups, width), F32), pltpu.VMEM((16, width), F32)]
         + [halves, halves, halves, pltpu.VMEM((groups, size // 2, width), BF16), halves, halves]
-        + [stack, stack, tall, tall, small, small, adds, adds, pltpu.VMEM((2, ntp - 1, rows, size), BF16)]
+        + [stack] * 4
+        + [tall, tall, small, small, adds, adds, pltpu.VMEM((2, ntp - 1, rows, size), BF16)]
         + [dma((2, chunks)), dma((2, ntp)), dma((2, ntp)), dma((nseq,)), dma((nseq,))]
         + [dma((2,)), dma((2,)), dma((groups,)), dma((groups,)), dma((2,)), dma((2,))]
         + [dma((2, ntp - 1, rows // CHUNK))] * 2,
@@ -411,14 +406,6 @@
         ),
         name="ssd_layer",
     )(head_inputs, out_grad, write_keys, read_queries, log_decay, skip_gain[None, :])
-    return pl.pallas_call(
-        store_kernel,
-        out_shape=tuple(jax.ShapeDtypeStruct(r.shape, r.dtype) for r in results),
-        in_specs=[vmem] * 4,
-        out_specs=[hbm] * 4,
-        scratch_shapes=[dma((4,))],
-        name="store_results",
-    )(*results)
 
 
 def solution(mesh):

time: 59.3 us -> 57.7 us (0.973)
  Pallas kernels: 53.9 us -> 52.3 us
    pallas_call x1 -> x0, Pallas kernels: 5.6 us -> none  [local(): pl.pallas_call(store_kernel, out_shape=tuple((jax.ShapeDtypeStruct(r.shap...]
    pallas_call x1, Pallas kernels: 48.3 us -> 52.3 us  [local(): pl.pallas_call(functools.partial(kernel, nseq, ntp), out_shape=(big, big,...]
    unnamed x8 -> x4, local copies, waits for them, and re-layouts: 4.57 us -> 4.59 us
where the time goes in v5:
time: 57.7 us; the launch traced here: 57.5 us
  Pallas kernels  52.3 us (91%)
  local copies, waits for them, and re-layouts  4.59 us (8%)
  between operations  0.64 us (1%)
    pallas_call x1, Pallas kernels, local(): pl.pallas_call(functools.partial(kernel, nseq, ntp), out_shape=(big, big,...  52.3 us
    unnamed x4, local copies, waits for them, and re-layouts  4.59 us

profile of v5, /device:TPU:0, one launch (start us, length us, event | category | flops | bytes accessed | tf_op | source)
XLA Modules:
  0.0 57.5 jit_solution(17921891664094044942)
XLA Ops:
  0.6 52.3 %ssd_layer.1 = (bf16[1024,1536]{1,0:T(8,128)(2,1)S(1)}, bf16[1024,1536]{1,0:T(8,128)(2,1)S(1)}, bf16[256,128]{1,0:T(8,128)(2,1)S(1)}, bf16[256,128]{1,0:T(8,128)(2,1)S(1)}) custom-call(bf16[1024,1536]{1,0:T(8,128)(2,1)} %x_hbm.1, bf16[1024,1536]{1,0:T(8,128)(2,1)} %g_hbm.1, bf16[256,128]{1,0:T(8,128)(2,1)} %k_ref.1, bf16[256,128]{1,0:T(8,128)(2,1)} %q_ref.1, ...), custom_call_target="tpu_custom_call" | custom-call | tf_op jit(solution)/shard_map/ssd_layer/pallas_call | solution.py:389
  52.9 1.7 %copy.14 = bf16[1024,1536]{1,0:T(8,128)(2,1)} copy(bf16[1024,1536]{1,0:T(8,128)(2,1)S(1)} %get-tuple-element.4) | data formatting | bytes 6291456
  54.6 0.6 %copy.16 = bf16[256,128]{1,0:T(8,128)(2,1)} copy(bf16[256,128]{1,0:T(8,128)(2,1)S(1)} %get-tuple-element.6) | data formatting | bytes 131072
  55.2 0.6 %copy.17 = bf16[256,128]{1,0:T(8,128)(2,1)} copy(bf16[256,128]{1,0:T(8,128)(2,1)S(1)} %get-tuple-element.7) | data formatting | bytes 131072
  55.9 1.7 %copy.15 = bf16[1024,1536]{1,0:T(8,128)(2,1)} copy(bf16[1024,1536]{1,0:T(8,128)(2,1)S(1)} %get-tuple-element.5) | data formatting | bytes 6291456

commit v6 on v3

--- a/solution.py
+++ b/solution.py
@@ -47,7 +47,7 @@
     mixed_ref, grad_ref, wout, rout,
     x_ref, g_ref, xs_ref, gs_ref, xe_ref, ge_ref, kbuf, qbuf, tsum, csum, factors, ea_ref, eb_ref,
     logsum, pairfac, corefac, pair_out, pair_in, sums_out, sums_in, half_out, half_in,
-    fstack, bstack, wpart, rpart, wlocal, rlocal, got,
+    fstack0, bstack0, fstack1, bstack1, wpart, rpart, wlocal, rlocal, got,
     load_sem, ag_send, ag_recv, log_send, log_recv, pair_send, pair_recv, sum_send, sum_recv,
     half_send, half_recv, rs_send, rs_recv,
 ):
@@ -144,15 +144,15 @@
     def scale(c, carry):
         at = rows_at(c, CHUNK)
         d = exact_nt(about_middle, ld_ref[:, at])
-        a, b = jnp.exp(-d), jnp.exp(d)
+        a, b = widen(jnp.exp(-d), width), widen(jnp.exp(d), width)
         ea_ref[at, :] = a
         eb_ref[at, :] = b
         load(0, c).wait()
-        x = x_ref[at, :].astype(F32) * widen(a, width)
+        x = x_ref[at, :].astype(F32) * a
         xs_ref[at, :] = x.astype(BF16)
         xe_ref[at, :] = (x * factor(0, c)).astype(BF16)
         load(1, c).wait()
-        g = g_ref[at, :].astype(F32) * widen(b, width)
+        g = g_ref[at, :].astype(F32) * b
         gs_ref[at, :] = g.astype(BF16)
         ge_ref[at, :] = (g * factor(1, c)).astype(BF16)
         return carry
@@ -297,8 +297,7 @@
             axis=0,
         )
         result = jnp.dot(both, stack[...], preferred_element_type=F32)
-        outer = widen(outer_ref[at, :], width)
-        out[at, :] = (outer * (result[:CHUNK] + skip * x.astype(F32))).astype(BF16)
+        out[at, :] = (outer_ref[at, :] * (result[:CHUNK] + skip * x.astype(F32))).astype(BF16)
         carry[...] = second * (low + result[CHUNK:])
         cross = lax.dot_general(b_ref[at, :], stack[CHUNK:, :], NT, preferred_element_type=F32)
         small[at, :] = (small_local[at, :] + cross).astype(BF16)
@@ -322,15 +321,25 @@
         def _():
             rs_copy(which, k, c - peer * per, c, peer).start()
 
-    def block(i, carry):
-        j = chunks - 1 - i
-        one(i, False, qbuf, kbuf, xs_ref, gs_ref, eb_ref, fstack, tsum, mixed_ref, rpart, rlocal)
-        one(j, True, kbuf, qbuf, gs_ref, xs_ref, ea_ref, bstack, csum, grad_ref, wpart, wlocal)
+    def forward(c, stack):
+        one(c, False, qbuf, kbuf, xs_ref, gs_ref, eb_ref, stack, tsum, mixed_ref, rpart, rlocal)
+
+    def backward(c, stack):
+        one(c, True, kbuf, qbuf, gs_ref, xs_ref, ea_ref, stack, csum, grad_ref, wpart, wlocal)
+
+    def two_blocks(m, carry):
+        i, j = 2 * m, chunks - 1 - 2 * m
+        forward(i, fstack0)
+        backward(j, bstack0)
+        forward(i + 1, fstack1)
+        backward(j - 1, bstack1)
         send_part(0, i)
         send_part(1, j)
+        send_part(0, i + 1)
+        send_part(1, j - 1)
         return carry
 
-    lax.fori_loop(0, chunks, block, 0)
+    lax.fori_loop(0, chunks // 2, two_blocks, 0)
 
     for which, (src, out) in enumerate(((rpart, rout), (wpart, wout))):
         total = src[own, :].astype(F32)
@@ -372,7 +381,7 @@
     small = pltpu.VMEM((tokens, size), F32)
     groups = nseq // 2
     lanes = -(-heads // LANES) * LANES
-    by_head = pltpu.VMEM((tokens, heads), F32)
+    outer = pltpu.VMEM((tokens, width), F32)
     stack = pltpu.VMEM((CHUNK + size, width), BF16)
     return pl.pallas_call(
         functools.partial(kernel, nseq, ntp),
@@ -380,11 +389,12 @@
         in_specs=[hbm, hbm, vmem, vmem, vmem, vmem],
         out_specs=[vmem] * 4,
         scratch_shapes=[wide] * 6
-        + [tall, tall, total, total, pltpu.VMEM((4 * chunks, width), F32), by_head, by_head]
+        + [tall, tall, total, total, pltpu.VMEM((4 * chunks, width), F32), outer, outer]
         + [pltpu.VMEM((nseq, 8, lanes), F32)]
         + [pltpu.VMEM((8 * groups, width), F32), pltpu.VMEM((16, width), F32)]
         + [halves, halves, halves, pltpu.VMEM((groups, size // 2, width), BF16), halves, halves]
-        + [stack, stack, tall, tall, small, small, pltpu.VMEM((2, ntp - 1, rows, size), BF16)]
+        + [stack] * 4
+        + [tall, tall, small, small, pltpu.VMEM((2, ntp - 1, rows, size), BF16)]
         + [dma((2, chunks)), dma((2, ntp)), dma((2, ntp)), dma((nseq,)), dma((nseq,))]
         + [dma((2,)), dma((2,)), dma((groups,)), dma((groups,)), dma((2,)), dma((2,))]
         + [dma((2, ntp - 1, rows // CHUNK))] * 2,

time: 53.7 us -> 55.2 us (1.028)
  Pallas kernels: 48.3 us -> 49.8 us
    pallas_call x1, Pallas kernels: 48.3 us -> 49.8 us  [local(): pl.pallas_call(functools.partial(kernel, nseq, ntp), out_shape=(big, big,...]
where the time goes in v6:
time: 55.2 us; the launch traced here: 55.1 us
  Pallas kernels  49.8 us (90%)
  local copies, waits for them, and re-layouts  4.59 us (8%)
  between operations  0.64 us (1%)
    pallas_call x1, Pallas kernels, local(): pl.pallas_call(functools.partial(kernel, nseq, ntp), out_shape=(big, big,...  49.8 us
    unnamed x4, local copies, waits for them, and re-layouts  4.59 us

profile of v6, /device:TPU:0, one launch (start us, length us, event | category | flops | bytes accessed | tf_op | source)
XLA Modules:
  0.0 55.1 jit_solution(5684180039281486103)
XLA Ops:
  0.6 49.8 %ssd_layer.1 = (bf16[1024,1536]{1,0:T(8,128)(2,1)S(1)}, bf16[1024,1536]{1,0:T(8,128)(2,1)S(1)}, bf16[256,128]{1,0:T(8,128)(2,1)S(1)}, bf16[256,128]{1,0:T(8,128)(2,1)S(1)}) custom-call(bf16[1024,1536]{1,0:T(8,128)(2,1)} %x_hbm.1, bf16[1024,1536]{1,0:T(8,128)(2,1)} %g_hbm.1, bf16[256,128]{1,0:T(8,128)(2,1)} %k_ref.1, bf16[256,128]{1,0:T(8,128)(2,1)} %q_ref.1, ...), custom_call_target="tpu_custom_call" | custom-call | tf_op jit(solution)/shard_map/ssd_layer/pallas_call | solution.py:386
  50.5 1.7 %copy.14 = bf16[1024,1536]{1,0:T(8,128)(2,1)} copy(bf16[1024,1536]{1,0:T(8,128)(2,1)S(1)} %get-tuple-element.4) | data formatting | bytes 6291456
  52.1 0.6 %copy.16 = bf16[256,128]{1,0:T(8,128)(2,1)} copy(bf16[256,128]{1,0:T(8,128)(2,1)S(1)} %get-tuple-element.6) | data formatting | bytes 131072
  52.8 0.6 %copy.17 = bf16[256,128]{1,0:T(8,128)(2,1)} copy(bf16[256,128]{1,0:T(8,128)(2,1)S(1)} %get-tuple-element.7) | data formatting | bytes 131072
  53.4 1.7 %copy.15 = bf16[1024,1536]{1,0:T(8,128)(2,1)} copy(bf16[1024,1536]{1,0:T(8,128)(2,1)S(1)} %get-tuple-element.5) | data formatting | bytes 6291456
